TPU v7x, 512 devices: a whole 4x4x16 slice. The times are simulated.
512 devices in a mesh: dp: 4 (over y), expert: 128 (over x, z, core).
Axes of the slice: x: 4, y: 4, z: 16, core: 2. Of those that a mesh axis runs over, the one named last changes fastest.
Arguments:
- down_cotangent: bfloat16 [65536, 2560], P(('dp', 'expert')), may hold values from -24 to 24
- saved_hidden: bfloat16 [65536, 6, 768], P(('dp', 'expert')), may hold values from -0.3125 to 0.3125
- route_ids: int32 [65536, 6], P(('dp', 'expert')), may hold values from 0 to 127, all different within a row; in each aligned block of 128 rows (0 to 127, 128 to 255, ...) at most 10 rows name the same one
- route_gates: bfloat16 [65536, 6], P(('dp', 'expert')), may hold values from 0.049804688 to 0.59765625
- down_weight: bfloat16 [128, 2560, 768], P('expert', 'dp'), may hold values from -0.21875 to 0.21875
Outputs:
- hidden_grad: bfloat16 [65536, 6, 768], P(('dp', 'expert'))
- gate_grad: bfloat16 [65536, 6], P(('dp', 'expert'))
- weight_grad: bfloat16 [128, 2560, 768], P('expert', 'dp')
Inputs may be any that keep to these rules, and one draw needn't show every extreme that they name: `route_ids`: each row names 6 different experts. Within the rows of one device (aligned blocks of 128 rows) no expert is named more than 10 times, and in some block one expert is named exactly 10 times.
All inputs are finite; a program needn't handle non-finite values.
Results may differ from a plain program's by a relative error of at most 0.013.
Values may be sent and summed in bfloat16 or wider, within the bound.
No kernel may reach another device: no remote copies, remote signals or barrier semaphores. Data moves between devices by JAX's collectives and lax.ppermute only.
A program may use at most 128 MiB of HBM per device.

v0:
```python
import jax
import jax.numpy as jnp
from jax import lax
from jax.sharding import PartitionSpec as P


def on_device(down_cotangent, saved_hidden, route_ids, route_gates, down_weight):
    tok_rows, top_count = route_ids.shape
    model_width = down_cotangent.shape[1]
    hidden = saved_hidden.shape[2]
    owner_count = lax.axis_size("expert")
    slot_count = min(tok_rows, 5 * tok_rows * top_count // (3 * owner_count))
    pair_count = tok_rows * top_count
    total_rows = owner_count * slot_count
    flat_ids = route_ids.reshape(pair_count)
    flat_gates = route_gates.reshape(pair_count)
    flat_hidden = saved_hidden.reshape(pair_count, hidden)
    onehot = (flat_ids[:, None] == jnp.arange(owner_count, dtype=jnp.int32)[None, :]).astype(
        jnp.int32
    )
    before = jnp.cumsum(onehot, axis=0) - onehot
    within = jnp.sum(before * onehot, axis=1)
    target = flat_ids * slot_count + within
    source = (
        jnp.full((total_rows,), pair_count, jnp.int32)
        .at[target]
        .set(jnp.arange(pair_count, dtype=jnp.int32))
    )
    filled = source < pair_count
    safe_rows = jnp.where(filled, source, 0)
    send_cot = jnp.where(filled[:, None], down_cotangent[safe_rows // top_count], 0)
    send_hid = jnp.where(filled[:, None], flat_hidden[safe_rows], 0)
    send_gate = jnp.where(filled, flat_gates[safe_rows], 0)
    got_cot, got_hid, got_gate = (
        lax.all_to_all(
            send_cot.reshape(owner_count, slot_count, model_width),
            "expert",
            split_axis=0,
            concat_axis=0,
            tiled=True,
        ),
        lax.all_to_all(
            send_hid.reshape(owner_count, slot_count, hidden),
            "expert",
            split_axis=0,
            concat_axis=0,
            tiled=True,
        ),
        lax.all_to_all(
            send_gate.reshape(owner_count, slot_count),
            "expert",
            split_axis=0,
            concat_axis=0,
            tiled=True,
        ),
    )
    work_cot = got_cot.reshape(total_rows, model_width)
    cols_part = work_cot
    grad_rows = jnp.dot(
        cols_part,
        lax.all_gather(down_weight[0], "dp", axis=0, tiled=True),
        preferred_element_type=jnp.float32,
    )
    work_hid = got_hid.reshape(total_rows, hidden)
    gate_float = got_gate.reshape(total_rows).astype(jnp.float32)
    slot_hidden = (gate_float[:, None] * grad_rows).astype(jnp.bfloat16)
    slot_gate = jnp.sum(grad_rows * work_hid.astype(jnp.float32), axis=1).astype(jnp.bfloat16)
    home_hidden, home_gate = (
        lax.all_to_all(
            slot_hidden.reshape(owner_count, slot_count, hidden),
            "expert",
            split_axis=0,
            concat_axis=0,
            tiled=True,
        ),
        lax.all_to_all(
            slot_gate.reshape(owner_count, slot_count),
            "expert",
            split_axis=0,
            concat_axis=0,
            tiled=True,
        ),
    )
    hidden_grad = home_hidden.reshape(total_rows, hidden)[target].reshape(
        tok_rows, top_count, hidden
    )
    gate_grad = home_gate.reshape(total_rows)[target].reshape(tok_rows, top_count)
    scaled = (gate_float[:, None] * work_hid.astype(jnp.float32)).astype(jnp.bfloat16)
    cols_part = work_cot
    total = lax.dot_general(
        cols_part, scaled, (((0,), (0,)), ((), ())), preferred_element_type=jnp.float32
    )
    rounded = lax.optimization_barrier(total.astype(jnp.bfloat16))
    weight_grad = lax.psum_scatter(
        rounded.astype(jnp.float32).astype(jnp.bfloat16), "dp", scatter_dimension=0, tiled=True
    ).astype(jnp.float32)
    return (hidden_grad, gate_grad, weight_grad[None].astype(jnp.bfloat16))


def solution(mesh):
    in_specs = (
        P(("dp", "expert"), None),
        P(("dp", "expert"), None, None),
        P(("dp", "expert"), None),
        P(("dp", "expert"), None),
        P("expert", "dp", None),
    )
    out_specs = (
        P(("dp", "expert"), None, None),
        P(("dp", "expert"), None),
        P("expert", "dp", None),
    )
    return jax.shard_map(
        on_device, mesh=mesh, in_specs=in_specs, out_specs=out_specs, check_vma=False
    )
```

profile of v0, /device:TPU:1, one launch (start us, length us, event | category | flops | bytes accessed | tf_op | source)
XLA Modules:
  0.0 914.9 jit_solution(11985188207301081111)
XLA Ops:
  7.2 0.9 copy.26
  8.0 0.1 eq.29
  8.3 0.7 broadcast_multiply_fusion
  9.1 0.2 fusion.7
  9.6 0.1 mul.41
  9.7 0.3 fusion.10
  10.1 3.4 scatter_custom_fusion
  13.5 0.8 copy.30
  14.3 0.2 reshape.133
  14.5 8.0 gather_fusion
  22.5 0.8 all_to_all.25
  23.3 20.4 %all-to-all-start = ((bf16[128,1,10]{2,1,0:T(2,128)(2,1)}), bf16[128,1,10]{2,1,0:T(2,128)(2,1)S(1)}, u32[]{:S(2)}, u32[]{:S(2)}) async-start(bf16[128,1,10]{2,1,0:T(2,128)(2,1)} %all_to_all.25), calls=%async_computation | async-start | bytes 131072 | tf_op jit(solution)/shard_map/all_to_all | solution.py:49
  43.7 0.2 broadcast_in_dim.53
  43.8 1.9 copy.32
  45.8 0.4 reshape.138
  46.2 4.9 gather_fusion.3
  51.1 4.7 gather.24
  55.8 3.3 broadcast_select_fusion.1
  59.1 16.6 %all-to-all-start.3 = ((bf16[128,10,768]{2,1,0:T(8,128)(2,1)}), bf16[128,10,768]{2,1,0:T(8,128)(2,1)}, u32[]{:S(2)}, u32[]{:S(2)}) async-start(bf16[128,10,768]{2,1,0:T(8,128)(2,1)} %broadcast_select_fusion.1), calls=%async_computation.3 | async-start | bytes 6291456 | tf_op jit(solution)/shard_map/all_to_all | solution.py:42
  75.8 6.6 gather_fusion.1
  82.4 12.5 %gather.21 = bf16[128,10,2560]{2,1,0:T(8,128)(2,1)} reshape(bf16[1280,2560]{1,0:T(8,128)(2,1)} %gather_fusion.1) | data formatting | bytes 13107200 | tf_op jit(solution)/shard_map/gather | solution.py:31
  94.9 9.9 %broadcast_select_fusion = bf16[128,10,2560]{2,1,0:T(8,128)(2,1)} fusion(bf16[128,10,2560]{2,1,0:T(8,128)(2,1)} %gather.21, pred[128,10]{1,0:T(8,128)(4,1)S(1)} %broadcast_in_dim.53), kind=kLoop, calls=%fused_computation.6 | loop fusion | flops 3276800 | bytes 13108480 | tf_op jit(solution)/shard_map/jit(_where)/select_n | solution.py:31
  104.7 113.5 %all-to-all-done.3 = bf16[128,10,768]{2,1,0:T(8,128)(2,1)} async-done(((bf16[128,10,768]{2,1,0:T(8,128)(2,1)}), bf16[128,10,768]{2,1,0:T(8,128)(2,1)}, u32[]{:S(2)}, u32[]{:S(2)}) %all-to-all-start.3) | async-done | bytes 1966112 | tf_op jit(solution)/shard_map/all_to_all | solution.py:42
  218.2 10.4 %all-to-all-start.1 = ((bf16[128,10,2560]{2,1,0:T(8,128)(2,1)}), bf16[128,10,2560]{2,1,0:T(8,128)(2,1)}, u32[]{:S(2)}, u32[]{:S(2)}) async-start(bf16[128,10,2560]{2,1,0:T(8,128)(2,1)} %broadcast_select_fusion), calls=%async_computation.1 | async-start | bytes 20971520 | tf_op jit(solution)/shard_map/all_to_all | solution.py:35
  228.7 0.7 all-gather.3.cloned.1.call-update
  229.4 0.2 convert_reduce_fusion
  229.6 0.1 reshape.141
  229.8 5.2 reshape.142
  235.0 4.1 multiply_convert_fusion
  239.1 444.4 %all-to-all-done.1 = bf16[128,10,2560]{2,1,0:T(8,128)(2,1)} async-done(((bf16[128,10,2560]{2,1,0:T(8,128)(2,1)}), bf16[128,10,2560]{2,1,0:T(8,128)(2,1)}, u32[]{:S(2)}, u32[]{:S(2)}) %all-to-all-start.1) | async-done | bytes 6553632 | tf_op jit(solution)/shard_map/all_to_all | solution.py:35
  683.5 12.7 %bitcast_convert_fusion = bf16[2560,768]{1,0:T(8,128)(2,1)} fusion(bf16[128,10,2560]{2,1,0:T(8,128)(2,1)} %all-to-all-done.1, bf16[128,10,768]{2,1,0:T(8,128)(2,1)} %multiply_convert_fusion), kind=kOutput, calls=%fused_computation.7 | convolution fusion | flops 5035130880 | bytes 12451840 | tf_op jit(solution)/shard_map/dot_general | solution.py:90
  696.2 12.8 %reshape.134 = bf16[1280,2560]{1,0:T(8,128)(2,1)} reshape(bf16[128,10,2560]{2,1,0:T(8,128)(2,1)} %all-to-all-done.1) | data formatting | bytes 13107200 | tf_op jit(solution)/shard_map/reshape | solution.py:57
  709.0 10.0 %multiply_reduce_fusion = (bf16[1280]{0:T(1024)(128)(2,1)S(1)}, bf16[1280,768]{1,0:T(8,128)(2,1)S(1)}) fusion(f32[1280,768]{1,0:T(8,128)} %reshape.142, f32[1280]{0:T(1024)S(1)} %reshape.141, bf16[1280,2560]{1,0:T(8,128)(2,1)} %reshape.134, bf16[1,2560,768]{2,1,0:T(8,128)(2,1)} %all-gather.3.cloned.1.call-done), kind=kOutput, calls=%fused_computation.13 | convolution fusion | flops 5037095936 | bytes 16391680 | tf_op jit(solution)/shard_map/dot_general | solution.py:59
  719.1 0.8 convert_element_type.88
  719.9 12.2 %all-to-all-start.4 = ((bf16[128,1,10]{2,1,0:T(2,128)(2,1)}), bf16[128,1,10]{2,1,0:T(2,128)(2,1)S(1)}, u32[]{:S(2)}, u32[]{:S(2)}) async-start(bf16[128,1,10]{2,1,0:T(2,128)(2,1)} %convert_element_type.88), calls=%async_computation.4 | async-start | bytes 131072 | tf_op jit(solution)/shard_map/all_to_all | solution.py:76
  732.0 2.4 reshape.135
  734.5 12.6 %all-to-all-done.4 = bf16[128,1,10]{2,1,0:T(2,128)(2,1)S(1)} async-done(((bf16[128,1,10]{2,1,0:T(2,128)(2,1)}), bf16[128,1,10]{2,1,0:T(2,128)(2,1)S(1)}, u32[]{:S(2)}, u32[]{:S(2)}) %all-to-all-start.4) | async-done | bytes 2592 | tf_op jit(solution)/shard_map/all_to_all | solution.py:76
  747.0 7.8 all-to-all-start.2
  754.9 0.2 reduce.2
  755.1 0.1 reshape.139
  755.2 5.0 gather_fusion.4
  760.2 0.1 reshape.140
  760.4 0.7 copy.37
  761.0 136.4 %all-to-all-done.2 = bf16[128,10,768]{2,1,0:T(8,128)(2,1)} async-done(((bf16[128,10,768]{2,1,0:T(8,128)(2,1)}), bf16[128,10,768]{2,1,0:T(8,128)(2,1)}, u32[]{:S(2)}, u32[]{:S(2)}) %all-to-all-start.2) | async-done | bytes 1966112 | tf_op jit(solution)/shard_map/all_to_all | solution.py:69
  897.4 3.7 reshape.136
  901.1 3.4 gather_fusion.2
  904.6 2.2 reshape.137
  906.8 1.2 copy.36
  (26 shorter events, 0.8 us)
Async XLA Ops:
  7.2 68.6 %copy-start = (bf16[128,2560]{1,0:T(8,128)(2,1)S(1)}, bf16[128,2560]{1,0:T(8,128)(2,1)}, u32[]{:S(2)}) copy-start(bf16[128,2560]{1,0:T(8,128)(2,1)} %param.5) | copy-start | bytes 1966084
  23.3 35.9 %all-to-all-start = ((bf16[128,1,10]{2,1,0:T(2,128)(2,1)}), bf16[128,1,10]{2,1,0:T(2,128)(2,1)S(1)}, u32[]{:S(2)}, u32[]{:S(2)}) async-start(bf16[128,1,10]{2,1,0:T(2,128)(2,1)} %all_to_all.25), calls=%async_computation | async-start | bytes 131072 | tf_op jit(solution)/shard_map/all_to_all | solution.py:49
  59.1 159.1 %all-to-all-start.3 = ((bf16[128,10,768]{2,1,0:T(8,128)(2,1)}), bf16[128,10,768]{2,1,0:T(8,128)(2,1)}, u32[]{:S(2)}, u32[]{:S(2)}) async-start(bf16[128,10,768]{2,1,0:T(8,128)(2,1)} %broadcast_select_fusion.1), calls=%async_computation.3 | async-start | bytes 6291456 | tf_op jit(solution)/shard_map/all_to_all | solution.py:42
  218.2 465.3 %all-to-all-start.1 = ((bf16[128,10,2560]{2,1,0:T(8,128)(2,1)}), bf16[128,10,2560]{2,1,0:T(8,128)(2,1)}, u32[]{:S(2)}, u32[]{:S(2)}) async-start(bf16[128,10,2560]{2,1,0:T(8,128)(2,1)} %broadcast_select_fusion), calls=%async_computation.1 | async-start | bytes 20971520 | tf_op jit(solution)/shard_map/all_to_all | solution.py:35
  228.6 480.4 %all-gather.3.cloned.1.call-start = ((), (), s32[]{:S(2)}) async-start(), calls=%async_computation.7 | async-start | bytes 4915200 | tf_op jit(solution)/shard_map/all_gather | solution.py:61
  229.3 678.7 %reduce-scatter.2.cloned.1.call-start = ((), (), s32[]{:S(2)}) async-start(), calls=%async_computation.6 | async-start | bytes 4915200 | tf_op jit(solution)/shard_map/reduce_scatter | solution.py:94
  719.9 27.2 %all-to-all-start.4 = ((bf16[128,1,10]{2,1,0:T(2,128)(2,1)}), bf16[128,1,10]{2,1,0:T(2,128)(2,1)S(1)}, u32[]{:S(2)}, u32[]{:S(2)}) async-start(bf16[128,1,10]{2,1,0:T(2,128)(2,1)} %convert_element_type.88), calls=%async_computation.4 | async-start | bytes 131072 | tf_op jit(solution)/shard_map/all_to_all | solution.py:76
  747.0 150.4 %all-to-all-start.2 = ((bf16[128,10,768]{2,1,0:T(8,128)(2,1)}), bf16[128,10,768]{2,1,0:T(8,128)(2,1)}, u32[]{:S(2)}, u32[]{:S(2)}) async-start(bf16[128,10,768]{2,1,0:T(8,128)(2,1)} %reshape.135), calls=%async_computation.2 | async-start | bytes 6291456 | tf_op jit(solution)/shard_map/all_to_all | solution.py:69
  901.1 6.9 copy-start.1
Sparse Core Ops, SparseCore 0:
  231.5 54.8 all-gather.2
  696.3 49.4 reduce-scatter.1
where the time goes:
time: 917 us; the launch traced here: 915 us
  waiting for transfers between devices  708 us (77%)
  local copies, waits for them, and re-layouts  83.8 us (9%)
  starting transfers between devices  67.5 us (7%)
  matrix products  22.7 us (2%)
  other arithmetic  19 us (2%)
  between operations  14.3 us (2%)
    all_to_all x1, waiting for transfers between devices, on_device(): lax.all_to_all(send_cot.reshape(owner_count, slot_count, model_width), 'e...  444 us
    all_to_all x1, waiting for transfers between devices, on_device(): lax.all_to_all(slot_hidden.reshape(owner_count, slot_count, hidden), 'exp...  136 us
    all_to_all x1, waiting for transfers between devices, on_device(): lax.all_to_all(send_hid.reshape(owner_count, slot_count, hidden), 'expert...  113 us
    all_to_all x1, starting transfers between devices, on_device(): lax.all_to_all(send_gate.reshape(owner_count, slot_count), 'expert', spli...  20.4 us
    gather x2, local copies, waits for them, and re-layouts, on_device(): down_cotangent[safe_rows // top_count]  19.1 us
  transfers between devices with their start and end apart: 7, of which 4 were waited for; matrix products, arithmetic and copies ran while one was open for 12% of the time, Pallas kernels for 0%

commit v1 on v0

v1 whole, which is shorter than its diff:
```python
import jax
import jax.numpy as jnp
from jax import lax
from jax.sharding import PartitionSpec as P

SLOTS = 10


def grid_of(dims):
    nx, nz, nc = dims
    along_z = [
        [(x * nz + z) * nc + c for z in range(nz)] for x in range(nx) for c in range(nc)
    ]
    in_plane = [
        [(x * nz + z) * nc + c for x in range(nx) for c in range(nc)] for z in range(nz)
    ]
    return along_z, in_plane


def on_device(dims, down_cotangent, saved_hidden, route_ids, route_gates, down_weight):
    nx, nz, nc = dims
    along_z, in_plane = grid_of(dims)
    experts, plane = nx * nz * nc, nx * nc
    tokens, top = route_ids.shape
    width, hidden = down_cotangent.shape[1], saved_hidden.shape[2]
    pairs, rows = tokens * top, experts * SLOTS
    lanes = SLOTS * hidden // 128

    ids = route_ids.T
    gates = route_gates.T.reshape(pairs, 1).astype(jnp.float32)
    hid = saved_hidden.transpose(1, 0, 2).reshape(pairs, hidden).astype(jnp.float32)

    named = ids[:, None, :] == jnp.arange(experts, dtype=jnp.int32)[None, :, None]
    member = jnp.any(named, axis=0)
    earlier = jnp.arange(tokens)[:, None] < jnp.arange(tokens)[None, :]
    rank = jnp.dot(
        member.astype(jnp.bfloat16),
        earlier.astype(jnp.bfloat16),
        preferred_element_type=jnp.float32,
    ).astype(jnp.int32)
    within = jnp.sum(jnp.where(named, rank[None], 0), axis=1)
    target = (ids * SLOTS + within).reshape(pairs)

    slot = jnp.arange(SLOTS, dtype=jnp.int32)
    table = jnp.max(
        jnp.where(
            member[:, None, :] & (rank[:, None, :] == slot[None, :, None]),
            jnp.arange(tokens, dtype=jnp.int32)[None, None, :],
            -1,
        ),
        axis=2,
    )
    table = table.reshape(nx, nz, nc * SLOTS).transpose(1, 0, 2).reshape(nz, 1, plane * SLOTS)

    table = lax.all_to_all(
        table, "expert", 0, 0, axis_index_groups=along_z, tiled=True
    ).reshape(nz, plane, SLOTS)

    replicas, replica = lax.axis_size("dp"), lax.axis_index("dp")
    own = down_weight[0]
    weight = jnp.zeros((replicas,) + own.shape, own.dtype)
    for step in range(replicas):
        block = own
        if step:
            block = lax.ppermute(
                own, "dp", [(i, (i - step) % replicas) for i in range(replicas)]
            )
        weight = lax.dynamic_update_index_in_dim(
            weight, block, (replica + step) % replicas, 0
        )
    weight = weight.reshape(width, hidden)

    scaled = (gates * hid).astype(jnp.bfloat16)
    send = (jnp.arange(rows, dtype=jnp.int32)[:, None] == target[None, :]).astype(jnp.bfloat16)
    sent = jnp.dot(send, scaled, preferred_element_type=jnp.float32).astype(jnp.bfloat16)
    sent = sent.reshape(experts, lanes, 128)

    line = lax.all_gather(
        down_cotangent, "expert", axis_index_groups=along_z, axis=0, tiled=True
    )
    line, sent, table, weight = lax.optimization_barrier((line, sent, table, weight))

    half = nz // 2
    line = line.reshape(2, half * tokens, width)
    place = lax.axis_index("expert")
    my_x, my_c = place // (nz * nc), place % nc
    offset = (jnp.arange(nz, dtype=jnp.int32) % half * tokens)[:, None, None]
    pick = jnp.where(table >= 0, table + offset, -1)
    pick = pick.reshape(2, half, nx, nc, SLOTS).transpose(2, 3, 0, 1, 4)
    pick = jnp.roll(jnp.roll(pick, -my_x, axis=0), -my_c, axis=1)
    pick = pick.reshape(plane, 2, half * SLOTS)
    choose = (
        pick[..., None] == jnp.arange(half * tokens, dtype=jnp.int32)[None, None, None, :]
    ).astype(jnp.bfloat16)
    chosen = jnp.einsum("dbrt,btw->dbrw", choose, line, preferred_element_type=jnp.float32)
    chosen = chosen.astype(jnp.bfloat16).reshape(plane, nz * SLOTS, width)
    work_cot, sources = [], []
    for dx in range(nx):
        for dc in range(nc):
            block = chosen[dx * nc + dc]
            if dx or dc:
                moves = [
                    ((x * nz + z) * nc + c, ((x + dx) % nx * nz + z) * nc + (c + dc) % nc)
                    for x in range(nx)
                    for z in range(nz)
                    for c in range(nc)
                ]
                block = lax.ppermute(block, "expert", moves)
            work_cot.append(block)
            sources.append((my_x - dx) % nx * nc + (my_c - dc) % nc)

    got = lax.all_to_all(sent, "expert", 0, 0, tiled=True)
    got = got.reshape(nx, nz, nc, lanes, 128).transpose(0, 2, 1, 3, 4)
    got = got.reshape(plane, nz * SLOTS, hidden)
    work_hid = jnp.concatenate(
        [lax.dynamic_index_in_dim(got, source, 0, keepdims=False) for source in sources]
    )

    back = jnp.zeros((plane, nz * SLOTS, hidden), jnp.bfloat16)
    for part, source in zip(work_cot, sources):
        grad_rows = jnp.dot(part, weight, preferred_element_type=jnp.float32)
        back = lax.dynamic_update_index_in_dim(back, grad_rows.astype(jnp.bfloat16), source, 0)
    back = back.reshape(nx, nc, nz, lanes, 128)
    back = back.transpose(0, 2, 1, 3, 4).reshape(experts, lanes, 128)
    home = lax.all_to_all(back, "expert", 0, 0, tiled=True).reshape(rows, hidden)

    total = lax.dot_general(
        jnp.concatenate(work_cot),
        work_hid,
        (((0,), (0,)), ((), ())),
        preferred_element_type=jnp.float32,
    ).astype(jnp.bfloat16)
    weight_grad = lax.psum_scatter(total, "dp", scatter_dimension=0, tiled=True)

    take = (target[:, None] == jnp.arange(rows, dtype=jnp.int32)[None, :]).astype(jnp.bfloat16)
    mine = jnp.dot(take, home, preferred_element_type=jnp.float32)
    hidden_grad = (gates * mine).astype(jnp.bfloat16)
    gate_grad = jnp.sum(mine * hid, axis=1).astype(jnp.bfloat16)
    hidden_grad = hidden_grad.reshape(top, tokens, hidden).transpose(1, 0, 2)
    return hidden_grad, gate_grad.reshape(top, tokens).T, weight_grad[None]


def solution(mesh):
    dims = (4, 16, 2)
    in_specs = (
        P(("dp", "expert"), None),
        P(("dp", "expert"), None, None),
        P(("dp", "expert"), None),
        P(("dp", "expert"), None),
        P("expert", "dp", None),
    )
    out_specs = (
        P(("dp", "expert"), None, None),
        P(("dp", "expert"), None),
        P("expert", "dp", None),
    )

    def step(*arrays):
        return on_device(dims, *arrays)

    return jax.shard_map(
        step, mesh=mesh, in_specs=in_specs, out_specs=out_specs, check_vma=False
    )
```

time: 917 us -> 424 us (0.46)
  waiting for transfers between devices: 708 us -> 234 us
  local copies, waits for them, and re-layouts: 83.8 us -> 48.7 us
  matrix products: 22.7 us -> 43.9 us
  other arithmetic: 19 us -> 2.8 us
  starting transfers between devices: 67.5 us -> 78.1 us
    all_to_all x5 -> x3, waiting for transfers between devices: 707 us -> 87.6 us  [the longest x1 83.4 us: on_device(): lax.all_to_all(back, 'expert', 0, 0, tiled=True).reshape(rows, hidden)]
    all_gather x1, waiting for transfers between devices: 0.01 us -> 78.6 us  [on_device(): lax.all_gather(down_cotangent, 'expert', axis_index_groups=along_z, axis=...]
    ppermute x0 -> x10, waiting for transfers between devices: none -> 67.4 us  [the longest x7 58 us: on_device(): block = lax.ppermute(block, 'expert', moves)]
    gather x7 -> x0, local copies, waits for them, and re-layouts: 45.1 us -> none  [the longest x2 19.1 us: on_device(): down_cotangent[safe_rows // top_count]]
    ppermute x0 -> x10, starting transfers between devices: none -> 34.9 us  [the longest x7 24.4 us: on_device(): block = lax.ppermute(block, 'expert', moves)]
    all_to_all x5 -> x3, starting transfers between devices: 67.4 us -> 43.2 us  [the longest x1 15.1 us: on_device(): lax.all_to_all(back, 'expert', 0, 0, tiled=True).reshape(rows, hidden)]
    dot_general x2 -> x13, matrix products: 22.7 us -> 43.9 us  [the longest x8 15.5 us: on_device(): grad_rows = jnp.dot(part, weight, preferred_element_type=jnp.float32)]
    select_n x6 -> x1, other arithmetic: 13.2 us -> 0.08 us  [on_device(): pick = jnp.where(table >= 0, table + offset, -1)]
  transfers between devices with their start and end apart: 7 -> 15, of which waited for: 4 -> 9; matrix products, arithmetic and copies ran while one was open for 12% -> 22% of each run, Pallas kernels for 0% -> 0%
where the time goes in v1:
time: 424 us; the launch traced here: 423 us
  waiting for transfers between devices  234 us (55%)
  starting transfers between devices  78.1 us (18%)
  local copies, waits for them, and re-layouts  48.7 us (11%)
  matrix products  43.9 us (10%)
  between operations  14.7 us (3%)
    all_to_all x1, waiting for transfers between devices, on_device(): lax.all_to_all(back, 'expert', 0, 0, tiled=True).reshape(rows, hidden)  83.4 us
    all_gather x1, waiting for transfers between devices, on_device(): lax.all_gather(down_cotangent, 'expert', axis_index_groups=along_z, axis=...  78.6 us
    ppermute x7, waiting for transfers between devices, on_device(): block = lax.ppermute(block, 'expert', moves)  58 us
    ppermute x7, starting transfers between devices, on_device(): block = lax.ppermute(block, 'expert', moves)  24.4 us
    dot_general x8, matrix products, on_device(): grad_rows = jnp.dot(part, weight, preferred_element_type=jnp.float32)  15.5 us
    all_to_all x1, starting transfers between devices, on_device(): lax.all_to_all(back, 'expert', 0, 0, tiled=True).reshape(rows, hidden)  15.1 us
    all_to_all x1, starting transfers between devices, on_device(): lax.all_to_all(table, 'expert', 0, 0, axis_index_groups=along_z, tiled=True)  14.9 us
    all_to_all x1, starting transfers between devices, on_device(): got = lax.all_to_all(sent, 'expert', 0, 0, tiled=True)  13.2 us
  transfers between devices with their start and end apart: 15, of which 9 were waited for; matrix products, arithmetic and copies ran while one was open for 22% of the time, Pallas kernels for 0%

profile of v1, /device:TPU:1, one launch (start us, length us, event | category | flops | bytes accessed | tf_op | source)
XLA Modules:
  0.0 422.6 jit_solution(10484096753032596166)
XLA Ops:
  7.9 5.6 %collective-permute-start = (bf16[640,768]{1,0:T(8,128)(2,1)}, bf16[640,768]{1,0:T(8,128)(2,1)}, u32[]{:S(2)}, u32[]{:S(2)}) collective-permute-start(bf16[640,768]{1,0:T(8,128)(2,1)} %bitcast.146), channel_id=1, source_target_pairs={{0,384},{128,0},{256,128},{384,256},{1,385},{129,1},{257,129},{385... | collective-permute-start | bytes 2949128 | tf_op jit(solution)/shard_map/ppermute | solution.py:65
  13.5 2.3 collective-permute-start.1
  15.8 2.6 collective-permute-start.2
  20.4 14.9 %all-to-all-start = ((s32[16,1,80]{2,1,0:T(1,128)}), s32[16,1,80]{2,1,0:T(1,128)S(1)}, u32[]{:S(2)}, u32[]{:S(2)}) async-start(s32[16,1,80]{2,1,0:T(1,128)} %bitcast.7), calls=%async_computation | async-start | bytes 16384 | tf_op jit(solution)/shard_map/all_to_all | solution.py:55
  37.7 1.9 fusion.2
  39.7 2.8 reshape.95
  42.5 4.3 %all-to-all-done = s32[16,1,80]{2,1,0:T(1,128)S(1)} async-done(((s32[16,1,80]{2,1,0:T(1,128)}), s32[16,1,80]{2,1,0:T(1,128)S(1)}, u32[]{:S(2)}, u32[]{:S(2)}) %all-to-all-start) | async-done | bytes 5152 | tf_op jit(solution)/shard_map/all_to_all | solution.py:55
  48.0 2.2 bitcast_dynamic-update-slice_fusion.2
  50.3 2.2 bitcast_dynamic-update-slice_fusion.1
  52.5 9.5 %collective-permute-done.2 = bf16[640,768]{1,0:T(8,128)(2,1)} collective-permute-done((bf16[640,768]{1,0:T(8,128)(2,1)}, bf16[640,768]{1,0:T(8,128)(2,1)}, u32[]{:S(2)}, u32[]{:S(2)}) %collective-permute-start.2) | collective-permute-done | bytes 983072 | tf_op jit(solution)/shard_map/ppermute | solution.py:65
  62.0 2.2 bitcast_dynamic-update-slice_fusion
  64.2 78.6 %all-gather.2.cloned.1.call-done = bf16[2048,2560]{1,0:T(8,128)(2,1)} async-done(((bf16[128,2560]{1,0:T(8,128)(2,1)}), bf16[2048,2560]{1,0:T(8,128)(2,1)}) %all-gather.2.cloned.1.call-update) | async-done | bytes 10485776 | tf_op jit(solution)/shard_map/all_gather | solution.py:78
  143.1 13.2 %all-to-all-start.2 = ((bf16[128,60,128]{2,1,0:T(8,128)(2,1)}), bf16[128,60,128]{2,1,0:T(8,128)(2,1)S(1)}, u32[]{:S(2)}, u32[]{:S(2)}) async-start(bf16[128,60,128]{2,1,0:T(8,128)(2,1)} %reshape.95), calls=%async_computation.2 | async-start | bytes 4194304 | tf_op jit(solution)/shard_map/all_to_all | solution.py:112
  156.3 13.1 %convert_bitcast_fusion = bf16[8,2,80,2560]{3,2,0,1:T(8,128)(2,1)} fusion(bf16[2,1024,2560,1]{2,1,3,0:T(8,128)(2,1)} %bitcast.159, s32[8,2,80]{2,0,1:T(8,128)S(1)} %copy.35), kind=kOutput, calls=%fused_computation | convolution fusion | flops 6715473920 | bytes 17044480 | tf_op jit(solution)/shard_map/dbrt,btw->dbrw/dot_general | solution.py:95
  169.3 5.5 %fusion.29 = (bf16[1,2,80,2560]{3,2,0,1:T(8,128)(2,1)}, bf16[1,2,80,2560]{3,2,0,1:T(8,128)(2,1)}, bf16[1,2,80,2560]{3,2,0,1:T(8,128)(2,1)}, bf16[1,2,80,2560]{3,...) fusion(bf16[8,2,80,2560]{3,2,0,1:T(8,128)(2,1)} %convert_bitcas, ...), kind=kLoop, calls=%fused_computation.81 | loop fusion | bytes 13107200 | tf_op jit(solution)/shard_map/slice | solution.py:100
  174.8 2.8 collective-permute-start.3
  177.8 2.9 collective-permute-start.4
  180.6 3.6 collective-permute-start.5
  184.3 3.3 collective-permute-start.6
  187.5 3.9 collective-permute-start.7
  192.4 1.4 broadcast_in_dim.88
  193.9 3.8 fusion.9
  197.7 3.3 collective-permute-start.8
  201.0 2.7 fusion.11
  203.7 2.1 collective-permute-done.4
  205.8 4.6 %collective-permute-start.9 = (bf16[160,2560]{1,0:T(8,128)(2,1)S(1)}, bf16[160,2560]{1,0:T(8,128)(2,1)S(1)}, u32[]{:S(2)}, u32[]{:S(2)}) collective-permute-start(bf16[160,2560]{1,0:T(8,128)(2,1)S(1)} %bitcast.149), channel_id=1, source_target_pairs={{0,97},{1,96},{2,99},{3,98},{4,101},{5,100},{6,103},{7,102},{8,105... | collective-permute-start | bytes 2457608 | tf_op jit(solution)/shard_map/ppermute | solution.py:108
  210.4 1.5 fusion.13
  211.9 17.3 %collective-permute-done.5 = bf16[160,2560]{1,0:T(8,128)(2,1)S(1)} collective-permute-done((bf16[160,2560]{1,0:T(8,128)(2,1)}, bf16[160,2560]{1,0:T(8,128)(2,1)S(1)}, u32[]{:S(2)}, u32[]{:S(2)}) %collective-permute-start.5) | collective-permute-done | bytes 819232 | tf_op jit(solution)/shard_map/ppermute | solution.py:108
  229.2 1.5 fusion.15
  230.7 22.1 %collective-permute-done.6 = bf16[160,2560]{1,0:T(8,128)(2,1)S(1)} collective-permute-done((bf16[160,2560]{1,0:T(8,128)(2,1)}, bf16[160,2560]{1,0:T(8,128)(2,1)S(1)}, u32[]{:S(2)}, u32[]{:S(2)}) %collective-permute-start.6) | collective-permute-done | bytes 819232 | tf_op jit(solution)/shard_map/ppermute | solution.py:108
  252.8 1.5 fusion.17
  254.4 16.3 %collective-permute-done.7 = bf16[160,2560]{1,0:T(8,128)(2,1)S(1)} collective-permute-done((bf16[160,2560]{1,0:T(8,128)(2,1)}, bf16[160,2560]{1,0:T(8,128)(2,1)S(1)}, u32[]{:S(2)}, u32[]{:S(2)}) %collective-permute-start.7) | collective-permute-done | bytes 819232 | tf_op jit(solution)/shard_map/ppermute | solution.py:108
  270.7 1.5 fusion.19
  272.2 1.5 fusion.21
  274.7 1.5 fusion.23
  276.2 4.4 %reshape.102 = bf16[4,2,16,60,128]{4,3,2,1,0:T(8,128)(2,1)} reshape(bf16[8,160,768]{2,1,0:T(8,128)(2,1)} %fusion.23) | data formatting | bytes 3932160 | tf_op jit(solution)/shard_map/reshape | solution.py:123
  280.6 3.6 copy.31
  284.3 2.6 copy.32
  286.9 2.3 constant_dynamic-update-slice_fusion.6
  289.2 1.0 constant_dynamic-update-slice_fusion.5
  293.0 1.0 constant_dynamic-update-slice_fusion.1
  294.9 15.1 %all-to-all-start.1 = ((bf16[128,60,128]{2,1,0:T(8,128)(2,1)}), bf16[128,60,128]{2,1,0:T(8,128)(2,1)}, u32[]{:S(2)}, u32[]{:S(2)}) async-start(bf16[128,60,128]{2,1,0:T(8,128)(2,1)} %copy.32), calls=%async_computation.1 | async-start | bytes 4194304 | tf_op jit(solution)/shard_map/all_to_all | solution.py:125
  310.0 1.6 copy.37
  311.7 3.5 reshape.107
  315.5 9.9 %convolution_convert_fusion = bf16[2560,768]{1,0:T(8,128)(2,1)} fusion(bf16[1280,2560]{1,0:T(8,128)(2,1)} %constant_dynamic-update-slice_fusion, bf16[1280,768]{1,0:T(8,128)(2,1)S(1)} %bitcast_dynamic-update-slice_fusion.3), kind=kOutput, calls=%fused_computation.2 | convolution fusion | flops 5035130880 | bytes 12451840 | tf_op jit(solution)/shard_map/dot_general | solution.py:127
  325.4 83.4 %all-to-all-done.1 = bf16[128,60,128]{2,1,0:T(8,128)(2,1)} async-done(((bf16[128,60,128]{2,1,0:T(8,128)(2,1)}), bf16[128,60,128]{2,1,0:T(8,128)(2,1)}, u32[]{:S(2)}, u32[]{:S(2)}) %all-to-all-start.1) | async-done | bytes 1966112 | tf_op jit(solution)/shard_map/all_to_all | solution.py:125
  408.8 3.5 reshape.104
  412.3 3.5 fusion.5
  (85 shorter events, 12.6 us)
Async XLA Ops:
  7.2 135.6 %all-gather.2.cloned.1.call-start = ((), (), s32[]{:S(2)}) async-start(), calls=%async_computation.4 | async-start | bytes 11141120 | tf_op jit(solution)/shard_map/all_gather | solution.py:78
  7.9 28.5 %copy-start.14 = (bf16[1,640,768]{2,1,0:T(8,128)(2,1)S(1)}, bf16[1,640,768]{2,1,0:T(8,128)(2,1)}, u32[]{:S(2)}) copy-start(bf16[1,640,768]{2,1,0:T(8,128)(2,1)} %param.9) | copy-start | bytes 2949124
  7.9 40.1 %collective-permute-start = (bf16[640,768]{1,0:T(8,128)(2,1)}, bf16[640,768]{1,0:T(8,128)(2,1)}, u32[]{:S(2)}, u32[]{:S(2)}) collective-permute-start(bf16[640,768]{1,0:T(8,128)(2,1)} %bitcast.146), channel_id=1, source_target_pairs={{0,384},{128,0},{256,128},{384,256},{1,385},{129,1},{257,129},{385... | collective-permute-start | bytes 2949128 | tf_op jit(solution)/shard_map/ppermute | solution.py:65
  13.5 36.7 %collective-permute-start.1 = (bf16[640,768]{1,0:T(8,128)(2,1)}, bf16[640,768]{1,0:T(8,128)(2,1)}, u32[]{:S(2)}, u32[]{:S(2)}) collective-permute-start(bf16[640,768]{1,0:T(8,128)(2,1)} %bitcast.147), channel_id=1, source_target_pairs={{0,256},{128,384},{256,0},{384,128},{1,257},{129,385},{257,1},{385... | collective-permute-start | bytes 2949128 | tf_op jit(solution)/shard_map/ppermute | solution.py:65
  15.8 46.2 %collective-permute-start.2 = (bf16[640,768]{1,0:T(8,128)(2,1)}, bf16[640,768]{1,0:T(8,128)(2,1)}, u32[]{:S(2)}, u32[]{:S(2)}) collective-permute-start(bf16[640,768]{1,0:T(8,128)(2,1)} %bitcast.148), channel_id=1, source_target_pairs={{0,128},{128,256},{256,384},{384,0},{1,129},{129,257},{257,385},{3... | collective-permute-start | bytes 2949128 | tf_op jit(solution)/shard_map/ppermute | solution.py:65
  20.4 26.3 %all-to-all-start = ((s32[16,1,80]{2,1,0:T(1,128)}), s32[16,1,80]{2,1,0:T(1,128)S(1)}, u32[]{:S(2)}, u32[]{:S(2)}) async-start(s32[16,1,80]{2,1,0:T(1,128)} %bitcast.7), calls=%async_computation | async-start | bytes 16384 | tf_op jit(solution)/shard_map/all_to_all | solution.py:55
  36.1 0.7 copy-start.18
  36.1 1.3 copy-start.12
  36.4 1.3 copy-start.17
  36.8 2.8 copy-start
  143.1 151.9 %all-to-all-start.2 = ((bf16[128,60,128]{2,1,0:T(8,128)(2,1)}), bf16[128,60,128]{2,1,0:T(8,128)(2,1)S(1)}, u32[]{:S(2)}, u32[]{:S(2)}) async-start(bf16[128,60,128]{2,1,0:T(8,128)(2,1)} %reshape.95), calls=%async_computation.2 | async-start | bytes 4194304 | tf_op jit(solution)/shard_map/all_to_all | solution.py:112
  174.8 22.8 %collective-permute-start.3 = (bf16[160,2560]{1,0:T(8,128)(2,1)}, bf16[160,2560]{1,0:T(8,128)(2,1)}, u32[]{:S(2)}, u32[]{:S(2)}) collective-permute-start(bf16[160,2560]{1,0:T(8,128)(2,1)} %bitcast.21), channel_id=1, source_target_pairs={{0,1},{1,0},{2,3},{3,2},{4,5},{5,4},{6,7},{7,6},{8,9},{9,8},{10,11... | collective-permute-start | bytes 2457608 | tf_op jit(solution)/shard_map/ppermute | solution.py:108
  177.8 28.0 %collective-permute-start.4 = (bf16[160,2560]{1,0:T(8,128)(2,1)}, bf16[160,2560]{1,0:T(8,128)(2,1)S(1)}, u32[]{:S(2)}, u32[]{:S(2)}) collective-permute-start(bf16[160,2560]{1,0:T(8,128)(2,1)} %bitcast.154), channel_id=1, source_target_pairs={{0,32},{1,33},{2,34},{3,35},{4,36},{5,37},{6,38},{7,39},{8,40},{9,... | collective-permute-start | bytes 2457608 | tf_op jit(solution)/shard_map/ppermute | solution.py:108
  180.6 48.6 %collective-permute-start.5 = (bf16[160,2560]{1,0:T(8,128)(2,1)}, bf16[160,2560]{1,0:T(8,128)(2,1)S(1)}, u32[]{:S(2)}, u32[]{:S(2)}) collective-permute-start(bf16[160,2560]{1,0:T(8,128)(2,1)} %bitcast.153), channel_id=1, source_target_pairs={{0,33},{1,32},{2,35},{3,34},{4,37},{5,36},{6,39},{7,38},{8,41},{9,... | collective-permute-start | bytes 2457608 | tf_op jit(solution)/shard_map/ppermute | solution.py:108
  184.3 68.6 %collective-permute-start.6 = (bf16[160,2560]{1,0:T(8,128)(2,1)}, bf16[160,2560]{1,0:T(8,128)(2,1)S(1)}, u32[]{:S(2)}, u32[]{:S(2)}) collective-permute-start(bf16[160,2560]{1,0:T(8,128)(2,1)} %bitcast.152), channel_id=1, source_target_pairs={{0,64},{1,65},{2,66},{3,67},{4,68},{5,69},{6,70},{7,71},{8,72},{9,... | collective-permute-start | bytes 2457608 | tf_op jit(solution)/shard_map/ppermute | solution.py:108
  187.5 83.1 %collective-permute-start.7 = (bf16[160,2560]{1,0:T(8,128)(2,1)}, bf16[160,2560]{1,0:T(8,128)(2,1)S(1)}, u32[]{:S(2)}, u32[]{:S(2)}) collective-permute-start(bf16[160,2560]{1,0:T(8,128)(2,1)} %bitcast.151), channel_id=1, source_target_pairs={{0,65},{1,64},{2,67},{3,66},{4,69},{5,68},{6,71},{7,70},{8,73},{9,... | collective-permute-start | bytes 2457608 | tf_op jit(solution)/shard_map/ppermute | solution.py:108
  193.9 3.8 copy-start.16
  193.9 7.1 %copy-start.1 = (bf16[4,640,768]{2,1,0:T(8,128)(2,1)S(1)}, bf16[4,640,768]{2,1,0:T(8,128)(2,1)}, u32[]{:S(2)}) copy-start(bf16[4,640,768]{2,1,0:T(8,128)(2,1)} %bitcast_dynamic-update-slice_fusion) | copy-start | bytes 11796484
  197.7 8.1 %copy-start.15 = (bf16[1,2,80,2560]{3,2,0,1:T(8,128)(2,1)S(1)}, bf16[1,2,80,2560]{3,2,0,1:T(8,128)(2,1)}, u32[]{:S(2)}) copy-start(bf16[1,2,80,2560]{3,2,0,1:T(8,128)(2,1)} %get-tuple-element.11) | copy-start | bytes 2457604
  197.7 74.5 %collective-permute-start.8 = (bf16[160,2560]{1,0:T(8,128)(2,1)S(1)}, bf16[160,2560]{1,0:T(8,128)(2,1)S(1)}, u32[]{:S(2)}, u32[]{:S(2)}) collective-permute-start(bf16[160,2560]{1,0:T(8,128)(2,1)S(1)} %bitcast.150), channel_id=1, source_target_pairs={{0,96},{1,97},{2,98},{3,99},{4,100},{5,101},{6,102},{7,103},{8,104... | collective-permute-start | bytes 2457608 | tf_op jit(solution)/shard_map/ppermute | solution.py:108
  205.7 6.2 %copy-start.2 = (bf16[160,2560]{1,0:T(8,128)(2,1)}, bf16[160,2560]{1,0:T(8,128)(2,1)S(1)}, u32[]{:S(2)}) copy-start(bf16[160,2560]{1,0:T(8,128)(2,1)S(1)} %collective-permute-done.4) | copy-start | bytes 2457604
  205.8 68.1 %collective-permute-start.9 = (bf16[160,2560]{1,0:T(8,128)(2,1)S(1)}, bf16[160,2560]{1,0:T(8,128)(2,1)S(1)}, u32[]{:S(2)}, u32[]{:S(2)}) collective-permute-start(bf16[160,2560]{1,0:T(8,128)(2,1)S(1)} %bitcast.149), channel_id=1, source_target_pairs={{0,97},{1,96},{2,99},{3,98},{4,101},{5,100},{6,103},{7,102},{8,105... | collective-permute-start | bytes 2457608 | tf_op jit(solution)/shard_map/ppermute | solution.py:108
  229.2 1.5 copy-start.4
  252.8 1.5 copy-start.6
  270.7 1.5 copy-start.8
  273.8 0.9 copy-start.10
  284.3 4.9 %copy-start.3 = (bf16[160,2560]{1,0:T(8,128)(2,1)S(1)}, bf16[160,2560]{1,0:T(8,128)(2,1)}, u32[]{:S(2)}) copy-start(bf16[160,2560]{1,0:T(8,128)(2,1)} %copy-done.2) | copy-start | bytes 2457604
  286.9 3.3 copy-start.5
  286.9 4.2 copy-start.7
  289.2 2.9 copy-start.9
  291.1 2.9 copy-start.11
  294.9 113.8 %all-to-all-start.1 = ((bf16[128,60,128]{2,1,0:T(8,128)(2,1)}), bf16[128,60,128]{2,1,0:T(8,128)(2,1)}, u32[]{:S(2)}, u32[]{:S(2)}) async-start(bf16[128,60,128]{2,1,0:T(8,128)(2,1)} %copy.32), calls=%async_computation.1 | async-start | bytes 4194304 | tf_op jit(solution)/shard_map/all_to_all | solution.py:125
  310.0 105.8 %reduce-scatter.2.cloned.1.call-start = ((), (), s32[]{:S(2)}) async-start(), calls=%async_computation.5 | async-start | bytes 4915200 | tf_op jit(solution)/shard_map/reduce_scatter | solution.py:133
  325.4 86.9 %copy-start.13 = (bf16[128,6,768]{2,0,1:T(8,128)(2,1)S(1)}, bf16[128,6,768]{2,0,1:T(8,128)(2,1)}, u32[]{:S(2)}) copy-start(bf16[128,6,768]{2,0,1:T(8,128)(2,1)} %param.6) | copy-start | bytes 3538948
Sparse Core Ops, SparseCore 0:
  10.1 132.6 all-gather.1
  325.5 53.3 reduce-scatter.1

commit v2 on v1

v2 whole, which is shorter than its diff:
```python
import jax
import jax.numpy as jnp
import numpy as np
from jax import lax
from jax.experimental import pallas as pl
from jax.experimental.pallas import tpu as pltpu
from jax.sharding import PartitionSpec as P

SLOTS = 10


def grid_of(dims):
    nx, nz, nc = dims
    along_z = [
        [(x * nz + z) * nc + c for z in range(nz)] for x in range(nx) for c in range(nc)
    ]
    in_plane = [
        [(x * nz + z) * nc + c for x in range(nx) for c in range(nc)] for z in range(nz)
    ]
    by_core = [
        [(x * nz + z) * nc + c for x in range(nx) for c in range(nc) for z in range(nz)]
    ]
    return along_z, in_plane, by_core


def picked_kernel(choose_ref, line_ref, *out_refs):
    rows = choose_ref.shape[1] // len(out_refs)
    for part in range(choose_ref.shape[0]):
        chosen = jnp.dot(
            choose_ref[part], line_ref[part], preferred_element_type=jnp.float32
        ).astype(jnp.bfloat16)
        for place, out_ref in enumerate(out_refs):
            out_ref[part * rows : (part + 1) * rows, :] = chosen[
                place * rows : (place + 1) * rows
            ]


def picked_rows(choose, line, places):
    parts, picks, depth = choose.shape
    width, tile = line.shape[2], 512
    out_rows = parts * picks // places
    return pl.pallas_call(
        picked_kernel,
        grid=(width // tile,),
        in_specs=[
            pl.BlockSpec((parts, picks, depth), lambda j: (0, 0, 0)),
            pl.BlockSpec((parts, depth, tile), lambda j: (0, 0, j)),
        ],
        out_specs=[pl.BlockSpec((out_rows, tile), lambda j: (0, j))] * places,
        out_shape=[jax.ShapeDtypeStruct((out_rows, width), jnp.bfloat16)] * places,
        compiler_params=pltpu.CompilerParams(vmem_limit_bytes=40 * 2**20),
        cost_estimate=pl.CostEstimate(
            flops=2 * parts * picks * depth * width,
            bytes_accessed=2 * (choose.size + line.size + parts * picks * width),
            transcendentals=0,
        ),
    )(choose, line)


def outer_kernel(*refs):
    *cot_refs, hid_ref, out_ref = refs
    out_ref[...] = lax.dot_general(
        jnp.concatenate([ref[...] for ref in cot_refs]),
        hid_ref[...],
        (((0,), (0,)), ((), ())),
        preferred_element_type=jnp.float32,
    ).astype(jnp.bfloat16)


def outer_sum(cot_parts, hid_rows):
    rows, hidden = hid_rows.shape
    width, tile = cot_parts[0].shape[1], 512
    return pl.pallas_call(
        outer_kernel,
        grid=(width // tile,),
        in_specs=[pl.BlockSpec((part.shape[0], tile), lambda j: (0, j)) for part in cot_parts]
        + [pl.BlockSpec((rows, hidden), lambda j: (0, 0))],
        out_specs=pl.BlockSpec((tile, hidden), lambda j: (j, 0)),
        out_shape=jax.ShapeDtypeStruct((width, hidden), jnp.bfloat16),
        compiler_params=pltpu.CompilerParams(vmem_limit_bytes=40 * 2**20),
        cost_estimate=pl.CostEstimate(
            flops=2 * rows * width * hidden,
            bytes_accessed=2 * (rows * (width + hidden) + width * hidden),
            transcendentals=0,
        ),
    )(*cot_parts, hid_rows)


def on_device(dims, down_cotangent, saved_hidden, route_ids, route_gates, down_weight):
    nx, nz, nc = dims
    along_z, in_plane, by_core = grid_of(dims)
    experts, plane = nx * nz * nc, nx * nc
    tokens, top = route_ids.shape
    width, hidden = down_cotangent.shape[1], saved_hidden.shape[2]
    pairs, rows = tokens * top, experts * SLOTS
    lanes = SLOTS * hidden // 128

    ids = route_ids.T
    gates = route_gates.T.reshape(pairs, 1).astype(jnp.float32)
    hid = saved_hidden.transpose(1, 0, 2).reshape(pairs, hidden).astype(jnp.float32)

    named = ids[:, None, :] == jnp.arange(experts, dtype=jnp.int32)[None, :, None]
    member = jnp.any(named, axis=0)
    earlier = jnp.arange(tokens)[:, None] < jnp.arange(tokens)[None, :]
    rank = jnp.dot(
        member.astype(jnp.bfloat16),
        earlier.astype(jnp.bfloat16),
        preferred_element_type=jnp.float32,
    ).astype(jnp.int32)
    within = jnp.sum(jnp.where(named, rank[None], 0), axis=1)

    slot = jnp.arange(SLOTS, dtype=jnp.int32)
    table = jnp.max(
        jnp.where(
            member[:, None, :] & (rank[:, None, :] == slot[None, :, None]),
            jnp.arange(tokens, dtype=jnp.int32)[None, None, :],
            -1,
        ),
        axis=2,
    )
    table = table.reshape(nx, nz, nc * SLOTS).transpose(1, 0, 2).reshape(nz, 1, plane * SLOTS)
    place = lax.axis_index("expert")
    my_x, my_z, my_c = place // (nz * nc), place // nc % nz, place % nc

    def permuted(source, block):
        pattern = source[:, None] == jnp.arange(block.shape[0], dtype=jnp.int32)[None, :]
        return jnp.dot(
            pattern.astype(jnp.bfloat16), block, preferred_element_type=jnp.float32
        ).astype(jnp.bfloat16)

    def swapped(block, groups):
        return lax.all_to_all(
            block, "expert", 0, 0, axis_index_groups=groups, tiled=True
        )

    replicas, replica = lax.axis_size("dp"), lax.axis_index("dp")
    own = down_weight[0]
    weight = jnp.zeros((replicas,) + own.shape, own.dtype)
    for step in range(replicas):
        block = own
        if step:
            block = lax.ppermute(
                own, "dp", [(i, (i - step) % replicas) for i in range(replicas)]
            )
        weight = lax.dynamic_update_index_in_dim(
            weight, block, (replica + step) % replicas, 0
        )
    weight = weight.reshape(width, hidden)

    scaled = (gates * hid).astype(jnp.bfloat16)
    ex, ez, ec = ids // (nz * nc), ids // nc % nz, ids % nc
    by_plane = (((ex * nc + ec) * nz + ez) * SLOTS + within).reshape(pairs)
    send = jnp.arange(rows, dtype=jnp.int32)[:, None] == by_plane[None, :]
    sent = jnp.dot(send.astype(jnp.bfloat16), scaled, preferred_element_type=jnp.float32)
    sent = swapped(sent.astype(jnp.bfloat16).reshape(plane, nz * SLOTS, hidden), in_plane)
    sent, table = lax.optimization_barrier((sent, table))
    table = swapped(table, along_z).reshape(nz, plane, SLOTS)
    order = np.arange(rows).reshape(plane, nz, SLOTS).transpose(1, 0, 2).reshape(rows)
    sent = permuted(jnp.asarray(order, jnp.int32), sent.reshape(rows, hidden))
    sent = sent.reshape(nz, plane * SLOTS, hidden)

    line = lax.all_gather(
        down_cotangent, "expert", axis_index_groups=along_z, axis=0, tiled=True
    )
    line, sent, table, weight = lax.optimization_barrier((line, sent, table, weight))

    work_hid = swapped(sent, along_z).reshape(rows, hidden)
    half = nz // 2
    line = line.reshape(2, half * tokens, width)
    offset = (jnp.arange(nz, dtype=jnp.int32) % half * tokens)[:, None, None]
    pick = jnp.where(table >= 0, table + offset, -1)
    pick = pick.reshape(2, half, nx, nc, SLOTS).transpose(2, 3, 0, 1, 4)
    pick = jnp.roll(jnp.roll(pick, -my_x, axis=0), -my_c, axis=1)
    pick = pick.reshape(plane, 2, half * SLOTS).transpose(1, 0, 2)
    pick = pick.reshape(2, plane * half * SLOTS, 1)
    token = jnp.arange(half * tokens, dtype=jnp.int32)
    choose = (pick == token).astype(jnp.bfloat16)
    chosen = picked_rows(choose, line, plane)

    work_cot = []
    back = jnp.zeros((plane, nz * SLOTS, hidden), jnp.bfloat16)
    for dx, dc in ((0, 0), (0, 1), (1, 0), (1, 1), (3, 0), (3, 1), (2, 0), (2, 1)):
        part = chosen[dx * nc + dc]
        if dx or dc:
            moves = [
                ((x * nz + z) * nc + c, ((x + dx) % nx * nz + z) * nc + (c + dc) % nc)
                for x in range(nx)
                for z in range(nz)
                for c in range(nc)
            ]
            part = lax.ppermute(part, "expert", moves)
        work_cot.append(part)
        grad_rows = jnp.dot(part, weight, preferred_element_type=jnp.float32)
        source = (my_x - dx) % nx * nc + (my_c - dc) % nc
        back = lax.dynamic_update_index_in_dim(back, grad_rows.astype(jnp.bfloat16), source, 0)
    home = swapped(back.reshape(experts, lanes, 128), by_core).reshape(rows, hidden)

    held = []
    for dx, dc in ((0, 0), (0, 1), (1, 0), (1, 1), (3, 0), (3, 1), (2, 0), (2, 1)):
        source = (my_x - dx) % nx * nc + (my_c - dc) % nc
        at = jnp.arange(nz * SLOTS, dtype=jnp.int32)
        held.append((at // SLOTS * plane + source) * SLOTS + at % SLOTS)
    total = outer_sum(work_cot, permuted(jnp.concatenate(held), work_hid))
    weight_grad = lax.psum_scatter(total, "dp", scatter_dimension=0, tiled=True)

    take = (by_plane[:, None] == jnp.arange(rows, dtype=jnp.int32)[None, :]).astype(jnp.bfloat16)
    mine = jnp.dot(take, home, preferred_element_type=jnp.float32)
    hidden_grad = (gates * mine).astype(jnp.bfloat16)
    gate_grad = jnp.sum(mine * hid, axis=1).astype(jnp.bfloat16)
    hidden_grad = hidden_grad.reshape(top, tokens, hidden).transpose(1, 0, 2)
    return hidden_grad, gate_grad.reshape(top, tokens).T, weight_grad[None]


def solution(mesh):
    dims = (4, 16, 2)
    in_specs = (
        P(("dp", "expert"), None),
        P(("dp", "expert"), None, None),
        P(("dp", "expert"), None),
        P(("dp", "expert"), None),
        P("expert", "dp", None),
    )
    out_specs = (
        P(("dp", "expert"), None, None),
        P(("dp", "expert"), None),
        P("expert", "dp", None),
    )

    def step(*arrays):
        return on_device(dims, *arrays)

    return jax.shard_map(
        step, mesh=mesh, in_specs=in_specs, out_specs=out_specs, check_vma=False
    )
```

time: 424 us -> 399 us (0.941)
  waiting for transfers between devices: 234 us -> 191 us
  local copies, waits for them, and re-layouts: 48.7 us -> 28.4 us
  Pallas kernels: 0 us -> 17.1 us
  starting transfers between devices: 78.1 us -> 91.1 us
    all_gather x1, waiting for transfers between devices: 78.6 us -> 38.2 us  [on_device(): lax.all_gather(down_cotangent, 'expert', axis_index_groups=along_z, axis=...]
    ppermute x7, waiting for transfers between devices: 58 us -> 29.3 us  [on_device(): part = lax.ppermute(part, 'expert', moves)]
    ppermute x3, waiting for transfers between devices: 9.48 us -> 33.7 us  [on_device(): lax.ppermute(own, 'dp', [(i, (i - step) % replicas) for i in range(replic...]
    pallas_call x0 -> x2, Pallas kernels: none -> 17.1 us  [the longest x1 10.3 us: picked_rows(): pl.pallas_call(picked_kernel, grid=(width // tile,), in_specs=[pl.BlockSp...]
    dot_general x8, matrix products: 15.5 us -> 29.9 us  [on_device(): grad_rows = jnp.dot(part, weight, preferred_element_type=jnp.float32)]
    all_to_all x3 -> x4, starting transfers between devices: 43.2 us -> 57.3 us  [swapped(): lax.all_to_all(block, 'expert', 0, 0, axis_index_groups=groups, tiled=True)]
    dot_general x3, matrix products: 24.8 us -> 12.1 us  [the longest x2 8.99 us: permuted(): jnp.dot(pattern.astype(jnp.bfloat16), block, preferred_element_type=jnp.f...]
    reshape x7 -> x5, local copies, waits for them, and re-layouts: 18.6 us -> 8.12 us  [the longest x1 4.43 us: on_device(): back.reshape(experts, lanes, 128)]
  transfers between devices with their start and end apart: 15 -> 16, of which waited for: 9 -> 8; matrix products, arithmetic and copies ran while one was open for 22% -> 18% of each run, Pallas kernels for 0% -> 4%
where the time goes in v2:
time: 399 us; the launch traced here: 394 us
  waiting for transfers between devices  191 us (48%)
  starting transfers between devices  91.1 us (23%)
  matrix products  45.7 us (11%)
  local copies, waits for them, and re-layouts  28.4 us (7%)
  Pallas kernels  17.1 us (4%)
  between operations  14.7 us (4%)
  other arithmetic  6 us (2%)
    all_to_all x4, waiting for transfers between devices, swapped(): lax.all_to_all(block, 'expert', 0, 0, axis_index_groups=groups, tiled=True)  89.4 us
    all_to_all x4, starting transfers between devices, swapped(): lax.all_to_all(block, 'expert', 0, 0, axis_index_groups=groups, tiled=True)  57.3 us
    all_gather x1, waiting for transfers between devices, on_device(): lax.all_gather(down_cotangent, 'expert', axis_index_groups=along_z, axis=...  38.2 us
    ppermute x3, waiting for transfers between devices, on_device(): lax.ppermute(own, 'dp', [(i, (i - step) % replicas) for i in range(replic...  33.7 us
    dot_general x8, matrix products, on_device(): grad_rows = jnp.dot(part, weight, preferred_element_type=jnp.float32)  29.9 us
    ppermute x7, waiting for transfers between devices, on_device(): part = lax.ppermute(part, 'expert', moves)  29.3 us
    ppermute x7, starting transfers between devices, on_device(): part = lax.ppermute(part, 'expert', moves)  22.4 us
    ppermute x3, starting transfers between devices, on_device(): lax.ppermute(own, 'dp', [(i, (i - step) % replicas) for i in range(replic...  11 us
  transfers between devices with their start and end apart: 16, of which 8 were waited for; matrix products, arithmetic and copies ran while one was open for 18% of the time, Pallas kernels for 4%

profile of v2, /device:TPU:1, one launch (start us, length us, event | category | flops | bytes accessed | tf_op | source)
XLA Modules:
  0.0 394.4 jit_solution(1239407348626369319)
XLA Ops:
  7.9 5.5 %collective-permute-start = (bf16[640,768]{1,0:T(8,128)(2,1)}, bf16[640,768]{1,0:T(8,128)(2,1)}, u32[]{:S(2)}, u32[]{:S(2)}) collective-permute-start(bf16[640,768]{1,0:T(8,128)(2,1)} %bitcast.104), channel_id=1, source_target_pairs={{0,384},{128,0},{256,128},{384,256},{1,385},{129,1},{257,129},{385... | collective-permute-start | bytes 2949128 | tf_op jit(solution)/shard_map/ppermute | solution.py:142
  16.4 1.5 fusion.10
  17.9 3.2 fusion.5
  21.1 7.0 %all-to-all-start = ((bf16[8,160,768]{2,1,0:T(8,128)(2,1)}), bf16[8,160,768]{2,1,0:T(8,128)(2,1)S(1)}, u32[]{:S(2)}, u32[]{:S(2)}) async-start(bf16[8,160,768]{2,1,0:T(8,128)(2,1)} %bitcast.103), calls=%async_computation | async-start | bytes 3932160 | tf_op jit(solution)/shard_map/all_to_all | solution.py:132
  28.1 1.9 collective-permute-start.1
  30.0 3.6 collective-permute-start.2
  34.8 2.2 broadcast_in_dim.95
  37.1 1.0 constant_dynamic-update-slice_fusion
  38.1 2.2 bitcast_dynamic-update-slice_fusion.2
  40.3 14.5 %collective-permute-done.1 = bf16[640,768]{1,0:T(8,128)(2,1)} collective-permute-done((bf16[640,768]{1,0:T(8,128)(2,1)S(1)}, bf16[640,768]{1,0:T(8,128)(2,1)}, u32[]{:S(2)}, u32[]{:S(2)}) %collective-permute-start.1) | collective-permute-done | bytes 983072 | tf_op jit(solution)/shard_map/ppermute | solution.py:142
  54.8 2.3 bitcast_dynamic-update-slice_fusion.1
  57.1 19.2 %collective-permute-done.2 = bf16[640,768]{1,0:T(8,128)(2,1)} collective-permute-done((bf16[640,768]{1,0:T(8,128)(2,1)S(1)}, bf16[640,768]{1,0:T(8,128)(2,1)}, u32[]{:S(2)}, u32[]{:S(2)}) %collective-permute-start.2) | collective-permute-done | bytes 983072 | tf_op jit(solution)/shard_map/ppermute | solution.py:142
  76.3 2.2 bitcast_dynamic-update-slice_fusion
  78.5 13.3 %all-to-all-start.1 = ((s32[16,1,80]{2,1,0:T(1,128)}), s32[16,1,80]{2,1,0:T(1,128)S(1)}, u32[]{:S(2)}, u32[]{:S(2)}) async-start(s32[16,1,80]{2,1,0:T(1,128)} %bitcast.10), calls=%async_computation.1 | async-start | bytes 16384 | tf_op jit(solution)/shard_map/all_to_all | solution.py:132
  91.9 4.3 %fusion.7 = bf16[1280,768]{1,0:T(8,128)(2,1)} fusion(bf16[1280,768]{1,0:T(8,128)(2,1)S(1)} %bitcast.102, s32[1280]{0:T(1024)S(1)} %copy-done.18), kind=kOutput, calls=%fused_computation.12 | convolution fusion | flops 2519203840 | bytes 3937280 | tf_op jit(solution)/shard_map/dot_general | solution.py:127
  96.2 7.1 %all-to-all-done.1 = s32[16,1,80]{2,1,0:T(1,128)S(1)} async-done(((s32[16,1,80]{2,1,0:T(1,128)}), s32[16,1,80]{2,1,0:T(1,128)S(1)}, u32[]{:S(2)}, u32[]{:S(2)}) %all-to-all-start.1) | async-done | bytes 5152 | tf_op jit(solution)/shard_map/all_to_all | solution.py:132
  104.6 38.2 %all-gather.2.cloned.1.call-done = bf16[2048,2560]{1,0:T(8,128)(2,1)} async-done(((bf16[128,2560]{1,0:T(8,128)(2,1)}), bf16[2048,2560]{1,0:T(8,128)(2,1)}) %all-gather.2.cloned.1.call-update) | async-done | bytes 10485776 | tf_op jit(solution)/shard_map/all_gather | solution.py:162
  142.8 8.6 %all-to-all-start.3 = ((bf16[16,80,768]{2,1,0:T(8,128)(2,1)}), bf16[16,80,768]{2,1,0:T(8,128)(2,1)}, u32[]{:S(2)}, u32[]{:S(2)}) async-start(bf16[16,80,768]{2,1,0:T(8,128)(2,1)} %bitcast.9), calls=%async_computation.3 | async-start | bytes 3932160 | tf_op jit(solution)/shard_map/all_to_all | solution.py:132
  152.4 10.3 %shard_map.85 = (bf16[160,2560]{1,0:T(8,128)(2,1)S(1)}, bf16[160,2560]{1,0:T(8,128)(2,1)}, bf16[160,2560]{1,0:T(8,128)(2,1)}, bf16[160,2560]{1,0:T(8,128)(2,1)S(...) custom-call(bf16[2,640,1024]{2,1,0:T(8,128)(2,1)S(1)} %fusion.2.choo, ...), custom_call_target="tpu_custom_call" | custom-call | flops 6710886400 | bytes 19660800 | tf_op jit(solution)/shard_map/pallas_call | solution.py:42
  165.4 0.9 copy-done.14
  166.3 0.9 copy-done.15
  167.2 2.8 collective-permute-start.3
  170.3 3.1 collective-permute-start.4
  173.5 3.3 collective-permute-start.5
  176.8 3.4 collective-permute-start.6
  180.2 2.6 collective-permute-start.7
  182.7 1.4 broadcast_in_dim.92
  184.2 3.7 fusion.15
  187.9 3.5 collective-permute-start.8
  191.4 3.6 fusion.17
  195.0 3.7 collective-permute-start.9
  198.8 3.6 fusion.19
  202.4 9.1 %collective-permute-done.5.refs_3_ = bf16[160,2560]{1,0:T(8,128)(2,1)S(1)} collective-permute-done((bf16[160,2560]{1,0:T(8,128)(2,1)}, bf16[160,2560]{1,0:T(8,128)(2,1)S(1)}, u32[]{:S(2)}, u32[]{:S(2)}) %collective-permute-start.5) | collective-permute-done | bytes 819232 | tf_op jit(solution)/shard_map/ppermute | solution.py:191
  211.5 3.6 fusion.21
  215.1 3.9 fusion.23
  219.1 3.9 fusion.25
  223.0 6.6 %collective-permute-done.8.refs_6_ = bf16[160,2560]{1,0:T(8,128)(2,1)S(1)} collective-permute-done((bf16[160,2560]{1,0:T(8,128)(2,1)S(1)}, bf16[160,2560]{1,0:T(8,128)(2,1)S(1)}, u32[]{:S(2)}, u32[]{:S(2)}) %collective-permute-start.8) | collective-permute-done | bytes 819232 | tf_op jit(solution)/shard_map/ppermute | solution.py:191
  229.6 3.9 fusion.27
  233.5 13.6 %collective-permute-done.9.refs_7_ = bf16[160,2560]{1,0:T(8,128)(2,1)S(1)} collective-permute-done((bf16[160,2560]{1,0:T(8,128)(2,1)S(1)}, bf16[160,2560]{1,0:T(8,128)(2,1)S(1)}, u32[]{:S(2)}, u32[]{:S(2)}) %collective-permute-start.9) | collective-permute-done | bytes 819232 | tf_op jit(solution)/shard_map/ppermute | solution.py:191
  247.1 3.6 fusion.29
  251.7 4.4 %reshape.94 = bf16[128,60,128]{2,1,0:T(8,128)(2,1)} reshape(bf16[8,160,768]{2,1,0:T(8,128)(2,1)} %fusion.29) | data formatting | bytes 3932160 | tf_op jit(solution)/shard_map/reshape | solution.py:196
  256.1 28.4 %all-to-all-start.2 = ((bf16[128,60,128]{2,1,0:T(8,128)(2,1)}), bf16[128,60,128]{2,1,0:T(8,128)(2,1)}, u32[]{:S(2)}, u32[]{:S(2)}) async-start(bf16[128,60,128]{2,1,0:T(8,128)(2,1)} %reshape.94), calls=%async_computation.2 | async-start | bytes 4194304 | tf_op jit(solution)/shard_map/all_to_all | solution.py:132
  284.8 4.7 %fusion.6.refs_8_ = bf16[1280,768]{1,0:T(8,128)(2,1)S(1)} fusion(bf16[1280,768]{1,0:T(8,128)(2,1)} %bitcast.33, s32[1280]{0:T(1024)S(1)} %concatenate.13), kind=kOutput, calls=%fused_computation.11 | convolution fusion | flops 2519203840 | bytes 3937280 | tf_op jit(solution)/shard_map/dot_general | solution.py:127
  289.5 6.8 %shard_map.86 = bf16[2560,768]{1,0:T(8,128)(2,1)S(1)} custom-call(bf16[160,2560]{1,0:T(8,128)(2,1)S(1)} %get-tuple-element.21.refs_0_, bf16[160,2560]{1,0:T(8,128)(2,1)S(1)} %collective-permute-done.3.refs_1_, bf16[160,2560]{1,0:T(8,128)(2,1)S(1)} %collective-permute-done.4.refs_2_, bf16[160,2560]{1,0:T(8,128)(2,1)S(1)} %collective-permute-done.5.refs_3_, ...), custom_call_target="tpu_custom_call" | custom-call | flops 5033164800 | bytes 12451840 | tf_op jit(solution)/shard_map/pallas_call | solution.py:73
  296.3 1.9 copy-done
  298.2 82.3 %all-to-all-done.2 = bf16[128,60,128]{2,1,0:T(8,128)(2,1)} async-done(((bf16[128,60,128]{2,1,0:T(8,128)(2,1)}), bf16[128,60,128]{2,1,0:T(8,128)(2,1)}, u32[]{:S(2)}, u32[]{:S(2)}) %all-to-all-start.2) | async-done | bytes 1966112 | tf_op jit(solution)/shard_map/all_to_all | solution.py:132
  380.6 3.5 reshape.95
  384.1 3.5 fusion.11
  (74 shorter events, 11.0 us)
Async XLA Ops:
  7.2 135.6 %all-gather.2.cloned.1.call-start = ((), (), s32[]{:S(2)}) async-start(), calls=%async_computation.5 | async-start | bytes 11141120 | tf_op jit(solution)/shard_map/all_gather | solution.py:162
  7.9 30.2 %collective-permute-start = (bf16[640,768]{1,0:T(8,128)(2,1)}, bf16[640,768]{1,0:T(8,128)(2,1)}, u32[]{:S(2)}, u32[]{:S(2)}) collective-permute-start(bf16[640,768]{1,0:T(8,128)(2,1)} %bitcast.104), channel_id=1, source_target_pairs={{0,384},{128,0},{256,128},{384,256},{1,385},{129,1},{257,129},{385... | collective-permute-start | bytes 2949128 | tf_op jit(solution)/shard_map/ppermute | solution.py:142
  21.1 7.0 %copy-start.17 = (bf16[1,640,768]{2,1,0:T(8,128)(2,1)S(1)}, bf16[1,640,768]{2,1,0:T(8,128)(2,1)}, u32[]{:S(2)}) copy-start(bf16[1,640,768]{2,1,0:T(8,128)(2,1)} %param.10) | copy-start | bytes 2949124
  21.1 57.4 %all-to-all-start = ((bf16[8,160,768]{2,1,0:T(8,128)(2,1)}), bf16[8,160,768]{2,1,0:T(8,128)(2,1)S(1)}, u32[]{:S(2)}, u32[]{:S(2)}) async-start(bf16[8,160,768]{2,1,0:T(8,128)(2,1)} %bitcast.103), calls=%async_computation | async-start | bytes 3932160 | tf_op jit(solution)/shard_map/all_to_all | solution.py:132
  28.1 26.8 %collective-permute-start.1 = (bf16[640,768]{1,0:T(8,128)(2,1)S(1)}, bf16[640,768]{1,0:T(8,128)(2,1)}, u32[]{:S(2)}, u32[]{:S(2)}) collective-permute-start(bf16[640,768]{1,0:T(8,128)(2,1)S(1)} %bitcast.105), channel_id=1, source_target_pairs={{0,256},{128,384},{256,0},{384,128},{1,257},{129,385},{257,1},{385... | collective-permute-start | bytes 2949128 | tf_op jit(solution)/shard_map/ppermute | solution.py:142
  30.0 46.4 %collective-permute-start.2 = (bf16[640,768]{1,0:T(8,128)(2,1)S(1)}, bf16[640,768]{1,0:T(8,128)(2,1)}, u32[]{:S(2)}, u32[]{:S(2)}) collective-permute-start(bf16[640,768]{1,0:T(8,128)(2,1)S(1)} %bitcast.106), channel_id=1, source_target_pairs={{0,128},{128,256},{256,384},{384,0},{1,129},{129,257},{257,385},{3... | collective-permute-start | bytes 2949128 | tf_op jit(solution)/shard_map/ppermute | solution.py:142
  40.3 51.6 %copy-start.18 = (s32[1280]{0:T(1024)S(1)}, s32[1280]{0:T(1024)}, u32[]{:S(2)}) copy-start(s32[1280]{0:T(1024)} %constant.324.clone) | copy-start | bytes 15364
  78.5 24.7 %all-to-all-start.1 = ((s32[16,1,80]{2,1,0:T(1,128)}), s32[16,1,80]{2,1,0:T(1,128)S(1)}, u32[]{:S(2)}, u32[]{:S(2)}) async-start(s32[16,1,80]{2,1,0:T(1,128)} %bitcast.10), calls=%async_computation.1 | async-start | bytes 16384 | tf_op jit(solution)/shard_map/all_to_all | solution.py:132
  142.8 113.3 %all-to-all-start.3 = ((bf16[16,80,768]{2,1,0:T(8,128)(2,1)}), bf16[16,80,768]{2,1,0:T(8,128)(2,1)}, u32[]{:S(2)}, u32[]{:S(2)}) async-start(bf16[16,80,768]{2,1,0:T(8,128)(2,1)} %bitcast.9), calls=%async_computation.3 | async-start | bytes 3932160 | tf_op jit(solution)/shard_map/all_to_all | solution.py:132
  162.7 0.9 copy-start.9
  163.6 0.9 copy-start.11
  164.5 0.9 copy-start.13
  165.4 0.9 copy-start.14
  166.3 0.9 copy-start.15
  167.2 20.7 %collective-permute-start.3 = (bf16[160,2560]{1,0:T(8,128)(2,1)}, bf16[160,2560]{1,0:T(8,128)(2,1)S(1)}, u32[]{:S(2)}, u32[]{:S(2)}) collective-permute-start(bf16[160,2560]{1,0:T(8,128)(2,1)} %get-tuple-element.23), channel_id=1, source_target_pairs={{0,1},{1,0},{2,3},{3,2},{4,5},{5,4},{6,7},{7,6},{8,9},{9,8},{10,11... | collective-permute-start | bytes 2457608 | tf_op jit(solution)/shard_map/ppermute | solution.py:191
  170.3 24.7 %collective-permute-start.4 = (bf16[160,2560]{1,0:T(8,128)(2,1)}, bf16[160,2560]{1,0:T(8,128)(2,1)S(1)}, u32[]{:S(2)}, u32[]{:S(2)}) collective-permute-start(bf16[160,2560]{1,0:T(8,128)(2,1)} %get-tuple-element.24), channel_id=1, source_target_pairs={{0,32},{1,33},{2,34},{3,35},{4,36},{5,37},{6,38},{7,39},{8,40},{9,... | collective-permute-start | bytes 2457608 | tf_op jit(solution)/shard_map/ppermute | solution.py:191
  173.5 38.0 %collective-permute-start.5 = (bf16[160,2560]{1,0:T(8,128)(2,1)}, bf16[160,2560]{1,0:T(8,128)(2,1)S(1)}, u32[]{:S(2)}, u32[]{:S(2)}) collective-permute-start(bf16[160,2560]{1,0:T(8,128)(2,1)} %copy-done.15), channel_id=1, source_target_pairs={{0,33},{1,32},{2,35},{3,34},{4,37},{5,36},{6,39},{7,38},{8,41},{9,... | collective-permute-start | bytes 2457608 | tf_op jit(solution)/shard_map/ppermute | solution.py:191
  176.8 38.4 %collective-permute-start.6 = (bf16[160,2560]{1,0:T(8,128)(2,1)}, bf16[160,2560]{1,0:T(8,128)(2,1)S(1)}, u32[]{:S(2)}, u32[]{:S(2)}) collective-permute-start(bf16[160,2560]{1,0:T(8,128)(2,1)} %copy-done.14), channel_id=1, source_target_pairs={{0,96},{1,97},{2,98},{3,99},{4,100},{5,101},{6,102},{7,103},{8,104... | collective-permute-start | bytes 2457608 | tf_op jit(solution)/shard_map/ppermute | solution.py:191
  180.2 38.9 %collective-permute-start.7 = (bf16[160,2560]{1,0:T(8,128)(2,1)}, bf16[160,2560]{1,0:T(8,128)(2,1)S(1)}, u32[]{:S(2)}, u32[]{:S(2)}) collective-permute-start(bf16[160,2560]{1,0:T(8,128)(2,1)} %copy-done.13), channel_id=1, source_target_pairs={{0,97},{1,96},{2,99},{3,98},{4,101},{5,100},{6,103},{7,102},{8,105... | collective-permute-start | bytes 2457608 | tf_op jit(solution)/shard_map/ppermute | solution.py:191
  184.2 3.7 copy-start.12
  187.9 7.2 %copy-start.10 = (bf16[160,2560]{1,0:T(8,128)(2,1)S(1)}, bf16[160,2560]{1,0:T(8,128)(2,1)}, u32[]{:S(2)}) copy-start(bf16[160,2560]{1,0:T(8,128)(2,1)} %copy-done.9) | copy-start | bytes 2457604
  187.9 41.7 %collective-permute-start.8 = (bf16[160,2560]{1,0:T(8,128)(2,1)S(1)}, bf16[160,2560]{1,0:T(8,128)(2,1)S(1)}, u32[]{:S(2)}, u32[]{:S(2)}) collective-permute-start(bf16[160,2560]{1,0:T(8,128)(2,1)S(1)} %copy-done.12), channel_id=1, source_target_pairs={{0,64},{1,65},{2,66},{3,67},{4,68},{5,69},{6,70},{7,71},{8,72},{9,... | collective-permute-start | bytes 2457608 | tf_op jit(solution)/shard_map/ppermute | solution.py:191
  195.0 52.1 %collective-permute-start.9 = (bf16[160,2560]{1,0:T(8,128)(2,1)S(1)}, bf16[160,2560]{1,0:T(8,128)(2,1)S(1)}, u32[]{:S(2)}, u32[]{:S(2)}) collective-permute-start(bf16[160,2560]{1,0:T(8,128)(2,1)S(1)} %copy-done.10), channel_id=1, source_target_pairs={{0,65},{1,64},{2,67},{3,66},{4,69},{5,68},{6,71},{7,70},{8,73},{9,... | collective-permute-start | bytes 2457608 | tf_op jit(solution)/shard_map/ppermute | solution.py:191
  215.1 3.9 copy-start.1
  219.1 3.9 copy-start.3
  229.6 3.9 copy-start.5
  250.8 0.9 copy-start.7
  256.1 124.5 %all-to-all-start.2 = ((bf16[128,60,128]{2,1,0:T(8,128)(2,1)}), bf16[128,60,128]{2,1,0:T(8,128)(2,1)}, u32[]{:S(2)}, u32[]{:S(2)}) async-start(bf16[128,60,128]{2,1,0:T(8,128)(2,1)} %reshape.94), calls=%async_computation.2 | async-start | bytes 4194304 | tf_op jit(solution)/shard_map/all_to_all | solution.py:132
  284.5 103.1 %reduce-scatter.2.cloned.1.call-start = ((), (), s32[]{:S(2)}) async-start(), calls=%async_computation.6 | async-start | bytes 4915200 | tf_op jit(solution)/shard_map/reduce_scatter | solution.py:204
  284.7 4.7 %copy-start.2 = (bf16[160,2560]{1,0:T(8,128)(2,1)S(1)}, bf16[160,2560]{1,0:T(8,128)(2,1)}, u32[]{:S(2)}) copy-start(bf16[160,2560]{1,0:T(8,128)(2,1)} %copy-done.1) | copy-start | bytes 2457604
  284.8 4.7 %copy-start.4 = (bf16[160,2560]{1,0:T(8,128)(2,1)S(1)}, bf16[160,2560]{1,0:T(8,128)(2,1)}, u32[]{:S(2)}) copy-start(bf16[160,2560]{1,0:T(8,128)(2,1)} %copy-done.3) | copy-start | bytes 2457604
  284.8 4.7 %copy-start.6 = (bf16[160,2560]{1,0:T(8,128)(2,1)S(1)}, bf16[160,2560]{1,0:T(8,128)(2,1)}, u32[]{:S(2)}) copy-start(bf16[160,2560]{1,0:T(8,128)(2,1)} %copy-done.5) | copy-start | bytes 2457604
  284.8 4.7 %copy-start.8 = (bf16[160,2560]{1,0:T(8,128)(2,1)S(1)}, bf16[160,2560]{1,0:T(8,128)(2,1)}, u32[]{:S(2)}) copy-start(bf16[160,2560]{1,0:T(8,128)(2,1)} %copy-done.7) | copy-start | bytes 2457604
  296.3 1.9 copy-start
  298.2 85.9 %copy-start.16 = (bf16[128,6,768]{2,0,1:T(8,128)(2,1)S(1)}, bf16[128,6,768]{2,0,1:T(8,128)(2,1)}, u32[]{:S(2)}) copy-start(bf16[128,6,768]{2,0,1:T(8,128)(2,1)} %param.7) | copy-start | bytes 3538948
Sparse Core Ops, SparseCore 0:
  10.1 132.6 all-gather.1
  298.3 53.2 reduce-scatter.1

commit v3 on v2

--- a/solution.py
+++ b/solution.py
@@ -7,6 +7,10 @@
 from jax.sharding import PartitionSpec as P
 
 SLOTS = 10
+GROUP = 4
+VMEM = 60 * 2**20
+PLACES = ((0, 0), (2, 0), (1, 0), (3, 0), (2, 1), (1, 1), (3, 1), (0, 1))
+DONE_ORDER = (0, 1, 2, 3, 4, 7, 6, 5)
 
 
 def grid_of(dims):
@@ -24,31 +28,30 @@
 
 
 def picked_kernel(choose_ref, line_ref, *out_refs):
-    rows = choose_ref.shape[1] // len(out_refs)
-    for part in range(choose_ref.shape[0]):
-        chosen = jnp.dot(
-            choose_ref[part], line_ref[part], preferred_element_type=jnp.float32
-        ).astype(jnp.bfloat16)
-        for place, out_ref in enumerate(out_refs):
-            out_ref[part * rows : (part + 1) * rows, :] = chosen[
-                place * rows : (place + 1) * rows
-            ]
+    lower, upper = [
+        jnp.dot(choose_ref[part], line_ref[part], preferred_element_type=jnp.float32)
+        for part in range(2)
+    ]
+    rows = lower.shape[0] // len(out_refs)
+    for place, out_ref in enumerate(out_refs):
+        chosen = slice(place * rows, (place + 1) * rows)
+        out_ref[...] = jnp.concatenate([lower[chosen], upper[chosen]]).astype(jnp.bfloat16)
 
 
 def picked_rows(choose, line, places):
     parts, picks, depth = choose.shape
-    width, tile = line.shape[2], 512
+    width, tile = line.shape[2], line.shape[2] // 2
     out_rows = parts * picks // places
     return pl.pallas_call(
         picked_kernel,
-        grid=(width // tile,),
+        grid=(parts // 2, width // tile),
         in_specs=[
-            pl.BlockSpec((parts, picks, depth), lambda j: (0, 0, 0)),
-            pl.BlockSpec((parts, depth, tile), lambda j: (0, 0, j)),
+            pl.BlockSpec((2, picks, depth), lambda i, j: (i, 0, 0)),
+            pl.BlockSpec((2, depth, tile), lambda i, j: (i, 0, j)),
         ],
-        out_specs=[pl.BlockSpec((out_rows, tile), lambda j: (0, j))] * places,
+        out_specs=[pl.BlockSpec((2 * picks // places, tile), lambda i, j: (i, j))] * places,
         out_shape=[jax.ShapeDtypeStruct((out_rows, width), jnp.bfloat16)] * places,
-        compiler_params=pltpu.CompilerParams(vmem_limit_bytes=40 * 2**20),
+        compiler_params=pltpu.CompilerParams(vmem_limit_bytes=VMEM),
         cost_estimate=pl.CostEstimate(
             flops=2 * parts * picks * depth * width,
             bytes_accessed=2 * (choose.size + line.size + parts * picks * width),
@@ -69,7 +72,7 @@
 
 def outer_sum(cot_parts, hid_rows):
     rows, hidden = hid_rows.shape
-    width, tile = cot_parts[0].shape[1], 512
+    width, tile = cot_parts[0].shape[1], 256
     return pl.pallas_call(
         outer_kernel,
         grid=(width // tile,),
@@ -77,7 +80,7 @@
         + [pl.BlockSpec((rows, hidden), lambda j: (0, 0))],
         out_specs=pl.BlockSpec((tile, hidden), lambda j: (j, 0)),
         out_shape=jax.ShapeDtypeStruct((width, hidden), jnp.bfloat16),
-        compiler_params=pltpu.CompilerParams(vmem_limit_bytes=40 * 2**20),
+        compiler_params=pltpu.CompilerParams(vmem_limit_bytes=VMEM),
         cost_estimate=pl.CostEstimate(
             flops=2 * rows * width * hidden,
             bytes_accessed=2 * (rows * (width + hidden) + width * hidden),
@@ -162,24 +165,21 @@
     line = lax.all_gather(
         down_cotangent, "expert", axis_index_groups=along_z, axis=0, tiled=True
     )
-    line, sent, table, weight = lax.optimization_barrier((line, sent, table, weight))
+    pick = jnp.where(
+        table >= 0, table + (jnp.arange(nz) % GROUP * tokens)[:, None, None], -1
+    )
+    pick = pick.reshape(nz, nx, nc, SLOTS).transpose(1, 2, 0, 3)
+    pick = jnp.roll(jnp.roll(pick, -my_x, axis=0), -my_c, axis=1)
+    pick = pick.reshape(plane, nz // GROUP, GROUP * SLOTS).transpose(1, 0, 2)
+    pick = pick.reshape(nz // GROUP, plane * GROUP * SLOTS, 1)
+    choose = (pick == jnp.arange(GROUP * tokens, dtype=jnp.int32)).astype(jnp.bfloat16)
+    line, sent, choose, weight = lax.optimization_barrier((line, sent, choose, weight))
 
     work_hid = swapped(sent, along_z).reshape(rows, hidden)
-    half = nz // 2
-    line = line.reshape(2, half * tokens, width)
-    offset = (jnp.arange(nz, dtype=jnp.int32) % half * tokens)[:, None, None]
-    pick = jnp.where(table >= 0, table + offset, -1)
-    pick = pick.reshape(2, half, nx, nc, SLOTS).transpose(2, 3, 0, 1, 4)
-    pick = jnp.roll(jnp.roll(pick, -my_x, axis=0), -my_c, axis=1)
-    pick = pick.reshape(plane, 2, half * SLOTS).transpose(1, 0, 2)
-    pick = pick.reshape(2, plane * half * SLOTS, 1)
-    token = jnp.arange(half * tokens, dtype=jnp.int32)
-    choose = (pick == token).astype(jnp.bfloat16)
-    chosen = picked_rows(choose, line, plane)
+    chosen = picked_rows(choose, line.reshape(nz // GROUP, GROUP * tokens, width), plane)
 
     work_cot = []
-    back = jnp.zeros((plane, nz * SLOTS, hidden), jnp.bfloat16)
-    for dx, dc in ((0, 0), (0, 1), (1, 0), (1, 1), (3, 0), (3, 1), (2, 0), (2, 1)):
+    for dx, dc in PLACES:
         part = chosen[dx * nc + dc]
         if dx or dc:
             moves = [
@@ -190,14 +190,17 @@
             ]
             part = lax.ppermute(part, "expert", moves)
         work_cot.append(part)
-        grad_rows = jnp.dot(part, weight, preferred_element_type=jnp.float32)
-        source = (my_x - dx) % nx * nc + (my_c - dc) % nc
-        back = lax.dynamic_update_index_in_dim(back, grad_rows.astype(jnp.bfloat16), source, 0)
+    sources = [(my_x - dx) % nx * nc + (my_c - dc) % nc for dx, dc in PLACES]
+    back = jnp.zeros((plane, nz * SLOTS, hidden), jnp.bfloat16)
+    for part in DONE_ORDER:
+        grads = jnp.dot(work_cot[part], weight, preferred_element_type=jnp.float32)
+        back = lax.dynamic_update_index_in_dim(
+            back, grads.astype(jnp.bfloat16), sources[part], 0
+        )
     home = swapped(back.reshape(experts, lanes, 128), by_core).reshape(rows, hidden)
 
     held = []
-    for dx, dc in ((0, 0), (0, 1), (1, 0), (1, 1), (3, 0), (3, 1), (2, 0), (2, 1)):
-        source = (my_x - dx) % nx * nc + (my_c - dc) % nc
+    for source in sources:
         at = jnp.arange(nz * SLOTS, dtype=jnp.int32)
         held.append((at // SLOTS * plane + source) * SLOTS + at % SLOTS)
     total = outer_sum(work_cot, permuted(jnp.concatenate(held), work_hid))

time: 399 us -> 378 us (0.947)
  local copies, waits for them, and re-layouts: 28.4 us -> 18.5 us
  starting transfers between devices: 91.1 us -> 83.5 us
  waiting for transfers between devices: 191 us -> 185 us
  Pallas kernels: 17.1 us -> 21.6 us
    all_to_all x4, starting transfers between devices: 57.3 us -> 44.1 us  [swapped(): lax.all_to_all(block, 'expert', 0, 0, axis_index_groups=groups, tiled=True)]
    unnamed x38 -> x22, local copies, waits for them, and re-layouts: 7.32 us -> 0.93 us
    ppermute x7, starting transfers between devices: 22.4 us -> 28.3 us  [on_device(): part = lax.ppermute(part, 'expert', moves)]
    pallas_call x1, Pallas kernels: 6.75 us -> 12.4 us  [outer_sum(): pl.pallas_call(outer_kernel, grid=(width // tile,), in_specs=[pl.BlockSpe...]
    dot_general x8, matrix products: 29.9 us -> 25.1 us  [on_device(): grads = jnp.dot(work_cot[part], weight, preferred_element_type=jnp.float32)]
    all_to_all x4, waiting for transfers between devices: 89.4 us -> 85.2 us  [swapped(): lax.all_to_all(block, 'expert', 0, 0, axis_index_groups=groups, tiled=True)]
  transfers between devices with their start and end apart: 16 -> 16, of which waited for: 8 -> 9; matrix products, arithmetic and copies ran while one was open for 18% -> 18% of each run, Pallas kernels for 4% -> 6%
where the time goes in v3:
time: 378 us; the launch traced here: 374 us
  waiting for transfers between devices  185 us (49%)
  starting transfers between devices  83.5 us (22%)
  matrix products  43.5 us (12%)
  Pallas kernels  21.6 us (6%)
  local copies, waits for them, and re-layouts  18.5 us (5%)
  between operations  14.7 us (4%)
  other arithmetic  7.04 us (2%)
    all_to_all x4, waiting for transfers between devices, swapped(): lax.all_to_all(block, 'expert', 0, 0, axis_index_groups=groups, tiled=True)  85.2 us
    all_to_all x4, starting transfers between devices, swapped(): lax.all_to_all(block, 'expert', 0, 0, axis_index_groups=groups, tiled=True)  44.1 us
    all_gather x1, waiting for transfers between devices, on_device(): lax.all_gather(down_cotangent, 'expert', axis_index_groups=along_z, axis=...  36.3 us
    ppermute x3, waiting for transfers between devices, on_device(): lax.ppermute(own, 'dp', [(i, (i - step) % replicas) for i in range(replic...  33.7 us
    ppermute x7, waiting for transfers between devices, on_device(): part = lax.ppermute(part, 'expert', moves)  28.9 us
    ppermute x7, starting transfers between devices, on_device(): part = lax.ppermute(part, 'expert', moves)  28.3 us
    dot_general x8, matrix products, on_device(): grads = jnp.dot(work_cot[part], weight, preferred_element_type=jnp.float32)  25.1 us
    pallas_call x1, Pallas kernels, outer_sum(): pl.pallas_call(outer_kernel, grid=(width // tile,), in_specs=[pl.BlockSpe...  12.4 us
  transfers between devices with their start and end apart: 16, of which 9 were waited for; matrix products, arithmetic and copies ran while one was open for 18% of the time, Pallas kernels for 6%

profile of v3, /device:TPU:1, one launch (start us, length us, event | category | flops | bytes accessed | tf_op | source)
XLA Modules:
  0.0 373.7 jit_solution(12957570016875476881)
XLA Ops:
  7.9 5.5 %collective-permute-start = (bf16[640,768]{1,0:T(8,128)(2,1)}, bf16[640,768]{1,0:T(8,128)(2,1)}, u32[]{:S(2)}, u32[]{:S(2)}) collective-permute-start(bf16[640,768]{1,0:T(8,128)(2,1)} %bitcast.101), channel_id=1, source_target_pairs={{0,384},{128,0},{256,128},{384,256},{1,385},{129,1},{257,129},{385... | collective-permute-start | bytes 2949128 | tf_op jit(solution)/shard_map/ppermute | solution.py:145
  13.4 0.7 fusion.31
  16.4 1.5 fusion.10
  17.9 3.2 fusion.4
  21.1 7.0 %all-to-all-start = ((bf16[8,160,768]{2,1,0:T(8,128)(2,1)}), bf16[8,160,768]{2,1,0:T(8,128)(2,1)S(1)}, u32[]{:S(2)}, u32[]{:S(2)}) async-start(bf16[8,160,768]{2,1,0:T(8,128)(2,1)} %bitcast.100), calls=%async_computation | async-start | bytes 3932160 | tf_op jit(solution)/shard_map/all_to_all | solution.py:135
  28.1 1.9 collective-permute-start.1
  30.0 3.6 collective-permute-start.2
  34.9 2.2 broadcast_in_dim.96
  37.1 1.0 constant_dynamic-update-slice_fusion
  38.2 2.2 bitcast_dynamic-update-slice_fusion.2
  40.4 14.4 %collective-permute-done.1 = bf16[640,768]{1,0:T(8,128)(2,1)} collective-permute-done((bf16[640,768]{1,0:T(8,128)(2,1)S(1)}, bf16[640,768]{1,0:T(8,128)(2,1)}, u32[]{:S(2)}, u32[]{:S(2)}) %collective-permute-start.1) | collective-permute-done | bytes 983072 | tf_op jit(solution)/shard_map/ppermute | solution.py:145
  54.8 2.3 bitcast_dynamic-update-slice_fusion.1
  57.1 19.2 %collective-permute-done.2 = bf16[640,768]{1,0:T(8,128)(2,1)} collective-permute-done((bf16[640,768]{1,0:T(8,128)(2,1)S(1)}, bf16[640,768]{1,0:T(8,128)(2,1)}, u32[]{:S(2)}, u32[]{:S(2)}) %collective-permute-start.2) | collective-permute-done | bytes 983072 | tf_op jit(solution)/shard_map/ppermute | solution.py:145
  76.4 2.2 bitcast_dynamic-update-slice_fusion
  78.6 13.3 %all-to-all-start.1 = ((s32[16,1,80]{2,1,0:T(1,128)}), s32[16,1,80]{2,1,0:T(1,128)S(1)}, u32[]{:S(2)}, u32[]{:S(2)}) async-start(s32[16,1,80]{2,1,0:T(1,128)} %bitcast.10), calls=%async_computation.1 | async-start | bytes 16384 | tf_op jit(solution)/shard_map/all_to_all | solution.py:135
  92.0 4.3 %fusion.6 = bf16[1280,768]{1,0:T(8,128)(2,1)} fusion(bf16[1280,768]{1,0:T(8,128)(2,1)S(1)} %bitcast.99, s32[1280]{0:T(1024)S(1)} %copy-done.10), kind=kOutput, calls=%fused_computation.10 | convolution fusion | flops 2519203840 | bytes 3937280 | tf_op jit(solution)/shard_map/dot_general | solution.py:130
  96.2 7.0 %all-to-all-done.1 = s32[16,1,80]{2,1,0:T(1,128)S(1)} async-done(((s32[16,1,80]{2,1,0:T(1,128)}), s32[16,1,80]{2,1,0:T(1,128)S(1)}, u32[]{:S(2)}, u32[]{:S(2)}) %all-to-all-start.1) | async-done | bytes 5152 | tf_op jit(solution)/shard_map/all_to_all | solution.py:135
  105.1 1.4 fusion.9.choose_ref
  106.4 36.3 %all-gather.2.cloned.1.call-done = bf16[2048,2560]{1,0:T(8,128)(2,1)} async-done(((bf16[128,2560]{1,0:T(8,128)(2,1)}), bf16[2048,2560]{1,0:T(8,128)(2,1)}) %all-gather.2.cloned.1.call-update) | async-done | bytes 10485776 | tf_op jit(solution)/shard_map/all_gather | solution.py:165
  142.8 8.6 %all-to-all-start.3 = ((bf16[16,80,768]{2,1,0:T(8,128)(2,1)}), bf16[16,80,768]{2,1,0:T(8,128)(2,1)}, u32[]{:S(2)}, u32[]{:S(2)}) async-start(bf16[16,80,768]{2,1,0:T(8,128)(2,1)} %bitcast.9), calls=%async_computation.3 | async-start | bytes 3932160 | tf_op jit(solution)/shard_map/all_to_all | solution.py:135
  151.4 9.2 %shard_map.85 = (bf16[160,2560]{1,0:T(8,128)(2,1)}, bf16[160,2560]{1,0:T(8,128)(2,1)}, bf16[160,2560]{1,0:T(8,128)(2,1)}, bf16[160,2560]{1,0:T(8,128)(2,1)}, bf1...) custom-call(bf16[4,320,512]{2,1,0:T(8,128)(2,1)} %fusion.9.choose_ref, ...), custom_call_target="tpu_custom_call" | custom-call | flops 3355443200 | bytes 18350080 | tf_op jit(solution)/shard_map/pallas_call | solution.py:45
  160.7 4.7 %collective-permute-start.3 = (bf16[160,2560]{1,0:T(8,128)(2,1)}, bf16[160,2560]{1,0:T(8,128)(2,1)}, u32[]{:S(2)}, u32[]{:S(2)}) collective-permute-start(bf16[160,2560]{1,0:T(8,128)(2,1)} %get-tuple-element.23), channel_id=1, source_target_pairs={{0,64},{1,65},{2,66},{3,67},{4,68},{5,69},{6,70},{7,71},{8,72},{9,... | collective-permute-start | bytes 2457608 | tf_op jit(solution)/shard_map/ppermute | solution.py:191
  165.6 2.2 collective-permute-start.4
  167.9 4.3 %collective-permute-start.5 = (bf16[160,2560]{1,0:T(8,128)(2,1)}, bf16[160,2560]{1,0:T(8,128)(2,1)S(1)}, u32[]{:S(2)}, u32[]{:S(2)}) collective-permute-start(bf16[160,2560]{1,0:T(8,128)(2,1)} %get-tuple-element.25), channel_id=1, source_target_pairs={{0,96},{1,97},{2,98},{3,99},{4,100},{5,101},{6,102},{7,103},{8,104... | collective-permute-start | bytes 2457608 | tf_op jit(solution)/shard_map/ppermute | solution.py:191
  172.2 2.7 collective-permute-start.6
  174.9 2.9 collective-permute-start.7
  178.0 3.0 fusion.15
  181.0 2.3 collective-permute-done.3.refs_1_
  183.3 7.7 %collective-permute-start.8 = (bf16[160,2560]{1,0:T(8,128)(2,1)S(1)}, bf16[160,2560]{1,0:T(8,128)(2,1)S(1)}, u32[]{:S(2)}, u32[]{:S(2)}) collective-permute-start(bf16[160,2560]{1,0:T(8,128)(2,1)S(1)} %copy-done.9), channel_id=1, source_target_pairs={{0,97},{1,96},{2,99},{3,98},{4,101},{5,100},{6,103},{7,102},{8,105... | collective-permute-start | bytes 2457608 | tf_op jit(solution)/shard_map/ppermute | solution.py:191
  191.0 3.2 fusion.17
  194.2 9.4 %collective-permute-done.4.refs_2_ = bf16[160,2560]{1,0:T(8,128)(2,1)} collective-permute-done((bf16[160,2560]{1,0:T(8,128)(2,1)}, bf16[160,2560]{1,0:T(8,128)(2,1)}, u32[]{:S(2)}, u32[]{:S(2)}) %collective-permute-start.4) | collective-permute-done | bytes 819232 | tf_op jit(solution)/shard_map/ppermute | solution.py:191
  203.5 3.8 %collective-permute-start.9 = (bf16[160,2560]{1,0:T(8,128)(2,1)S(1)}, bf16[160,2560]{1,0:T(8,128)(2,1)S(1)}, u32[]{:S(2)}, u32[]{:S(2)}) collective-permute-start(bf16[160,2560]{1,0:T(8,128)(2,1)S(1)} %copy-done.8), channel_id=1, source_target_pairs={{0,33},{1,32},{2,35},{3,34},{4,37},{5,36},{6,39},{7,38},{8,41},{9,... | collective-permute-start | bytes 2457608 | tf_op jit(solution)/shard_map/ppermute | solution.py:191
  207.4 3.2 fusion.19
  210.6 3.2 fusion.21
  213.8 7.6 %collective-permute-done.6.refs_4_ = bf16[160,2560]{1,0:T(8,128)(2,1)S(1)} collective-permute-done((bf16[160,2560]{1,0:T(8,128)(2,1)}, bf16[160,2560]{1,0:T(8,128)(2,1)S(1)}, u32[]{:S(2)}, u32[]{:S(2)}) %collective-permute-start.6) | collective-permute-done | bytes 819232 | tf_op jit(solution)/shard_map/ppermute | solution.py:191
  221.4 3.2 fusion.23
  224.7 3.2 fusion.25
  227.9 9.6 %collective-permute-done.8.refs_6_ = bf16[160,2560]{1,0:T(8,128)(2,1)S(1)} collective-permute-done((bf16[160,2560]{1,0:T(8,128)(2,1)S(1)}, bf16[160,2560]{1,0:T(8,128)(2,1)S(1)}, u32[]{:S(2)}, u32[]{:S(2)}) %collective-permute-start.8) | collective-permute-done | bytes 819232 | tf_op jit(solution)/shard_map/ppermute | solution.py:191
  237.5 3.2 fusion.27
  240.8 0.9 copy-done.7
  241.7 2.9 fusion.29
  244.6 2.8 reshape.92
  247.4 15.1 %all-to-all-start.2 = ((bf16[128,60,128]{2,1,0:T(8,128)(2,1)}), bf16[128,60,128]{2,1,0:T(8,128)(2,1)S(1)}, u32[]{:S(2)}, u32[]{:S(2)}) async-start(bf16[128,60,128]{2,1,0:T(8,128)(2,1)} %reshape.92), calls=%async_computation.2 | async-start | bytes 4194304 | tf_op jit(solution)/shard_map/all_to_all | solution.py:135
  262.6 5.8 %fusion.5.refs_8_ = bf16[1280,768]{1,0:T(8,128)(2,1)} fusion(bf16[1280,768]{1,0:T(8,128)(2,1)} %bitcast.32, s32[1280]{0:T(1024)S(1)} %concatenate.13), kind=kOutput, calls=%fused_computation.9 | convolution fusion | flops 2519203840 | bytes 3937280 | tf_op jit(solution)/shard_map/dot_general | solution.py:130
  268.4 12.4 %shard_map.86 = bf16[2560,768]{1,0:T(8,128)(2,1)} custom-call(bf16[160,2560]{1,0:T(8,128)(2,1)} %get-tuple-element.21.refs_0_, bf16[160,2560]{1,0:T(8,128)(2,1)} %collective-permute-done.3.refs_1_, bf16[160,2560]{1,0:T(8,128)(2,1)} %collective-permute-done.4.refs_2_, bf16[160,2560]{1,0:T(8,128)(2,1)} %copy-done.3, bf16[160,2560]{1,0:T(8,128)(2,1)} %copy-done.4, ...), custom_call_target="tpu_custom_call" | custom-call | flops 5033164800 | bytes 12451840 | tf_op jit(solution)/shard_map/pallas_call | solution.py:76
  280.8 78.2 %all-to-all-done.2 = bf16[128,60,128]{2,1,0:T(8,128)(2,1)S(1)} async-done(((bf16[128,60,128]{2,1,0:T(8,128)(2,1)}), bf16[128,60,128]{2,1,0:T(8,128)(2,1)S(1)}, u32[]{:S(2)}, u32[]{:S(2)}) %all-to-all-start.2) | async-done | bytes 1966112 | tf_op jit(solution)/shard_map/all_to_all | solution.py:135
  359.0 2.8 reshape.93
  361.8 5.0 %fusion.11 = (bf16[768]{0:T(1024)(128)(2,1)}, bf16[768,768]{1,0:T(8,128)(2,1)}) fusion(bf16[128,6,768]{2,0,1:T(8,128)(2,1)S(1)} %copy-done, f32[768]{0:T(1024)S(1)} %convert_bitcast_fusion, bf16[1280,768]{1,0:T(8,128)(2,1)} %reshape.93, s32[768]{0:T(1024)S(1)} %fusion.42), kind=kOutput, calls=%fused_computation.18 | convolution fusion | flops 1513880832 | bytes 4333056 | tf_op jit(solution)/shard_map/dot_general | solution.py:210
  (58 shorter events, 6.3 us)
Async XLA Ops:
  7.2 135.6 %all-gather.2.cloned.1.call-start = ((), (), s32[]{:S(2)}) async-start(), calls=%async_computation.5 | async-start | bytes 11141120 | tf_op jit(solution)/shard_map/all_gather | solution.py:165
  7.9 30.3 %collective-permute-start = (bf16[640,768]{1,0:T(8,128)(2,1)}, bf16[640,768]{1,0:T(8,128)(2,1)}, u32[]{:S(2)}, u32[]{:S(2)}) collective-permute-start(bf16[640,768]{1,0:T(8,128)(2,1)} %bitcast.101), channel_id=1, source_target_pairs={{0,384},{128,0},{256,128},{384,256},{1,385},{129,1},{257,129},{385... | collective-permute-start | bytes 2949128 | tf_op jit(solution)/shard_map/ppermute | solution.py:145
  21.1 7.0 %copy-start.1 = (bf16[1,640,768]{2,1,0:T(8,128)(2,1)S(1)}, bf16[1,640,768]{2,1,0:T(8,128)(2,1)}, u32[]{:S(2)}) copy-start(bf16[1,640,768]{2,1,0:T(8,128)(2,1)} %param.10) | copy-start | bytes 2949124
  21.1 57.5 %all-to-all-start = ((bf16[8,160,768]{2,1,0:T(8,128)(2,1)}), bf16[8,160,768]{2,1,0:T(8,128)(2,1)S(1)}, u32[]{:S(2)}, u32[]{:S(2)}) async-start(bf16[8,160,768]{2,1,0:T(8,128)(2,1)} %bitcast.100), calls=%async_computation | async-start | bytes 3932160 | tf_op jit(solution)/shard_map/all_to_all | solution.py:135
  28.1 26.8 %collective-permute-start.1 = (bf16[640,768]{1,0:T(8,128)(2,1)S(1)}, bf16[640,768]{1,0:T(8,128)(2,1)}, u32[]{:S(2)}, u32[]{:S(2)}) collective-permute-start(bf16[640,768]{1,0:T(8,128)(2,1)S(1)} %bitcast.102), channel_id=1, source_target_pairs={{0,256},{128,384},{256,0},{384,128},{1,257},{129,385},{257,1},{385... | collective-permute-start | bytes 2949128 | tf_op jit(solution)/shard_map/ppermute | solution.py:145
  30.0 46.4 %collective-permute-start.2 = (bf16[640,768]{1,0:T(8,128)(2,1)S(1)}, bf16[640,768]{1,0:T(8,128)(2,1)}, u32[]{:S(2)}, u32[]{:S(2)}) collective-permute-start(bf16[640,768]{1,0:T(8,128)(2,1)S(1)} %bitcast.103), channel_id=1, source_target_pairs={{0,128},{128,256},{256,384},{384,0},{1,129},{129,257},{257,385},{3... | collective-permute-start | bytes 2949128 | tf_op jit(solution)/shard_map/ppermute | solution.py:145
  40.4 51.6 %copy-start.10 = (s32[1280]{0:T(1024)S(1)}, s32[1280]{0:T(1024)}, u32[]{:S(2)}) copy-start(s32[1280]{0:T(1024)} %constant.287.clone) | copy-start | bytes 15364
  78.6 24.6 %all-to-all-start.1 = ((s32[16,1,80]{2,1,0:T(1,128)}), s32[16,1,80]{2,1,0:T(1,128)S(1)}, u32[]{:S(2)}, u32[]{:S(2)}) async-start(s32[16,1,80]{2,1,0:T(1,128)} %bitcast.10), calls=%async_computation.1 | async-start | bytes 16384 | tf_op jit(solution)/shard_map/all_to_all | solution.py:135
  142.8 104.6 %all-to-all-start.3 = ((bf16[16,80,768]{2,1,0:T(8,128)(2,1)}), bf16[16,80,768]{2,1,0:T(8,128)(2,1)}, u32[]{:S(2)}, u32[]{:S(2)}) async-start(bf16[16,80,768]{2,1,0:T(8,128)(2,1)} %bitcast.9), calls=%async_computation.3 | async-start | bytes 3932160 | tf_op jit(solution)/shard_map/all_to_all | solution.py:135
  160.6 17.3 %copy-start.2 = (bf16[160,2560]{1,0:T(8,128)(2,1)S(1)}, bf16[160,2560]{1,0:T(8,128)(2,1)}, u32[]{:S(2)}) copy-start(bf16[160,2560]{1,0:T(8,128)(2,1)} %get-tuple-element.21.refs_0_) | copy-start | bytes 2457604
  160.7 22.7 %collective-permute-start.3 = (bf16[160,2560]{1,0:T(8,128)(2,1)}, bf16[160,2560]{1,0:T(8,128)(2,1)}, u32[]{:S(2)}, u32[]{:S(2)}) collective-permute-start(bf16[160,2560]{1,0:T(8,128)(2,1)} %get-tuple-element.23), channel_id=1, source_target_pairs={{0,64},{1,65},{2,66},{3,67},{4,68},{5,69},{6,70},{7,71},{8,72},{9,... | collective-permute-start | bytes 2457608 | tf_op jit(solution)/shard_map/ppermute | solution.py:191
  165.6 37.9 %collective-permute-start.4 = (bf16[160,2560]{1,0:T(8,128)(2,1)}, bf16[160,2560]{1,0:T(8,128)(2,1)}, u32[]{:S(2)}, u32[]{:S(2)}) collective-permute-start(bf16[160,2560]{1,0:T(8,128)(2,1)} %get-tuple-element.24), channel_id=1, source_target_pairs={{0,32},{1,33},{2,34},{3,35},{4,36},{5,37},{6,38},{7,39},{8,40},{9,... | collective-permute-start | bytes 2457608 | tf_op jit(solution)/shard_map/ppermute | solution.py:191
  167.9 42.7 %collective-permute-start.5 = (bf16[160,2560]{1,0:T(8,128)(2,1)}, bf16[160,2560]{1,0:T(8,128)(2,1)S(1)}, u32[]{:S(2)}, u32[]{:S(2)}) collective-permute-start(bf16[160,2560]{1,0:T(8,128)(2,1)} %get-tuple-element.25), channel_id=1, source_target_pairs={{0,96},{1,97},{2,98},{3,99},{4,100},{5,101},{6,102},{7,103},{8,104... | collective-permute-start | bytes 2457608 | tf_op jit(solution)/shard_map/ppermute | solution.py:191
  172.2 49.2 %collective-permute-start.6 = (bf16[160,2560]{1,0:T(8,128)(2,1)}, bf16[160,2560]{1,0:T(8,128)(2,1)S(1)}, u32[]{:S(2)}, u32[]{:S(2)}) collective-permute-start(bf16[160,2560]{1,0:T(8,128)(2,1)} %get-tuple-element.26), channel_id=1, source_target_pairs={{0,65},{1,64},{2,67},{3,66},{4,69},{5,68},{6,71},{7,70},{8,73},{9,... | collective-permute-start | bytes 2457608 | tf_op jit(solution)/shard_map/ppermute | solution.py:191
  174.9 49.7 %collective-permute-start.7 = (bf16[160,2560]{1,0:T(8,128)(2,1)}, bf16[160,2560]{1,0:T(8,128)(2,1)S(1)}, u32[]{:S(2)}, u32[]{:S(2)}) collective-permute-start(bf16[160,2560]{1,0:T(8,128)(2,1)} %get-tuple-element.27), channel_id=1, source_target_pairs={{0,1},{1,0},{2,3},{3,2},{4,5},{5,4},{6,7},{7,6},{8,9},{9,8},{10,11... | collective-permute-start | bytes 2457608 | tf_op jit(solution)/shard_map/ppermute | solution.py:191
  178.0 5.3 %copy-start.9 = (bf16[160,2560]{1,0:T(8,128)(2,1)S(1)}, bf16[160,2560]{1,0:T(8,128)(2,1)}, u32[]{:S(2)}) copy-start(bf16[160,2560]{1,0:T(8,128)(2,1)} %get-tuple-element.28) | copy-start | bytes 2457604
  183.3 20.2 %copy-start.8 = (bf16[160,2560]{1,0:T(8,128)(2,1)S(1)}, bf16[160,2560]{1,0:T(8,128)(2,1)}, u32[]{:S(2)}) copy-start(bf16[160,2560]{1,0:T(8,128)(2,1)} %get-tuple-element.29) | copy-start | bytes 2457604
  183.3 54.2 %collective-permute-start.8 = (bf16[160,2560]{1,0:T(8,128)(2,1)S(1)}, bf16[160,2560]{1,0:T(8,128)(2,1)S(1)}, u32[]{:S(2)}, u32[]{:S(2)}) collective-permute-start(bf16[160,2560]{1,0:T(8,128)(2,1)S(1)} %copy-done.9), channel_id=1, source_target_pairs={{0,97},{1,96},{2,99},{3,98},{4,101},{5,100},{6,103},{7,102},{8,105... | collective-permute-start | bytes 2457608 | tf_op jit(solution)/shard_map/ppermute | solution.py:191
  203.5 37.2 %collective-permute-start.9 = (bf16[160,2560]{1,0:T(8,128)(2,1)S(1)}, bf16[160,2560]{1,0:T(8,128)(2,1)S(1)}, u32[]{:S(2)}, u32[]{:S(2)}) collective-permute-start(bf16[160,2560]{1,0:T(8,128)(2,1)S(1)} %copy-done.8), channel_id=1, source_target_pairs={{0,33},{1,32},{2,35},{3,34},{4,37},{5,36},{6,39},{7,38},{8,41},{9,... | collective-permute-start | bytes 2457608 | tf_op jit(solution)/shard_map/ppermute | solution.py:191
  210.6 3.2 copy-start.3
  221.4 3.2 copy-start.4
  224.7 3.2 copy-start.5
  237.5 3.2 copy-start.6
  240.8 0.9 copy-start.7
  247.4 111.6 %all-to-all-start.2 = ((bf16[128,60,128]{2,1,0:T(8,128)(2,1)}), bf16[128,60,128]{2,1,0:T(8,128)(2,1)S(1)}, u32[]{:S(2)}, u32[]{:S(2)}) async-start(bf16[128,60,128]{2,1,0:T(8,128)(2,1)} %reshape.92), calls=%async_computation.2 | async-start | bytes 4194304 | tf_op jit(solution)/shard_map/all_to_all | solution.py:135
  262.6 104.3 %reduce-scatter.2.cloned.1.call-start = ((), (), s32[]{:S(2)}) async-start(), calls=%async_computation.6 | async-start | bytes 4915200 | tf_op jit(solution)/shard_map/reduce_scatter | solution.py:207
  280.8 81.0 %copy-start = (bf16[128,6,768]{2,0,1:T(8,128)(2,1)S(1)}, bf16[128,6,768]{2,0,1:T(8,128)(2,1)}, u32[]{:S(2)}) copy-start(bf16[128,6,768]{2,0,1:T(8,128)(2,1)} %param.7) | copy-start | bytes 3538948
Sparse Core Ops, SparseCore 0:
  10.1 132.6 all-gather.1
  280.9 53.2 reduce-scatter.1

commit v4 on v3

--- a/solution.py
+++ b/solution.py
@@ -10,7 +10,7 @@
 GROUP = 4
 VMEM = 60 * 2**20
 PLACES = ((0, 0), (2, 0), (1, 0), (3, 0), (2, 1), (1, 1), (3, 1), (0, 1))
-DONE_ORDER = (0, 1, 2, 3, 4, 7, 6, 5)
+DONE_ORDER = (0, 1, 2, 3, 4, 7, 5, 6)
 
 
 def grid_of(dims):
@@ -197,7 +197,9 @@
         back = lax.dynamic_update_index_in_dim(
             back, grads.astype(jnp.bfloat16), sources[part], 0
         )
-    home = swapped(back.reshape(experts, lanes, 128), by_core).reshape(rows, hidden)
+    take = (by_plane[:, None] == jnp.arange(rows, dtype=jnp.int32)[None, :]).astype(jnp.bfloat16)
+    take, back = lax.optimization_barrier((take, back))
+    home = swapped(back.reshape(experts, lanes // 4, 4, 128), by_core).reshape(rows, hidden)
 
     held = []
     for source in sources:
@@ -206,7 +208,6 @@
     total = outer_sum(work_cot, permuted(jnp.concatenate(held), work_hid))
     weight_grad = lax.psum_scatter(total, "dp", scatter_dimension=0, tiled=True)
 
-    take = (by_plane[:, None] == jnp.arange(rows, dtype=jnp.int32)[None, :]).astype(jnp.bfloat16)
     mine = jnp.dot(take, home, preferred_element_type=jnp.float32)
     hidden_grad = (gates * mine).astype(jnp.bfloat16)
     gate_grad = jnp.sum(mine * hid, axis=1).astype(jnp.bfloat16)

time: 378 us -> 371 us (0.981)
  waiting for transfers between devices: 185 us -> 179 us
    all_to_all x4, waiting for transfers between devices: 85.2 us -> 78.9 us  [swapped(): lax.all_to_all(block, 'expert', 0, 0, axis_index_groups=groups, tiled=True)]
  transfers between devices with their start and end apart: 16 -> 16, of which waited for: 9 -> 9; matrix products, arithmetic and copies ran while one was open for 18% -> 19% of each run, Pallas kernels for 6% -> 6%
where the time goes in v4:
time: 371 us; the launch traced here: 366 us
  waiting for transfers between devices  179 us (48%)
  starting transfers between devices  81.6 us (22%)
  matrix products  43.9 us (12%)
  Pallas kernels  21.6 us (6%)
  local copies, waits for them, and re-layouts  16.1 us (4%)
  between operations  14.7 us (4%)
  other arithmetic  8.72 us (2%)
    all_to_all x4, waiting for transfers between devices, swapped(): lax.all_to_all(block, 'expert', 0, 0, axis_index_groups=groups, tiled=True)  78.9 us
    all_to_all x4, starting transfers between devices, swapped(): lax.all_to_all(block, 'expert', 0, 0, axis_index_groups=groups, tiled=True)  44.3 us
    all_gather x1, waiting for transfers between devices, on_device(): lax.all_gather(down_cotangent, 'expert', axis_index_groups=along_z, axis=...  36.3 us
    ppermute x3, waiting for transfers between devices, on_device(): lax.ppermute(own, 'dp', [(i, (i - step) % replicas) for i in range(replic...  33.8 us
    ppermute x7, waiting for transfers between devices, on_device(): part = lax.ppermute(part, 'expert', moves)  29.5 us
    ppermute x7, starting transfers between devices, on_device(): part = lax.ppermute(part, 'expert', moves)  26.2 us
    dot_general x8, matrix products, on_device(): grads = jnp.dot(work_cot[part], weight, preferred_element_type=jnp.float32)  25.1 us
    pallas_call x1, Pallas kernels, outer_sum(): pl.pallas_call(outer_kernel, grid=(width // tile,), in_specs=[pl.BlockSpe...  12.4 us
  transfers between devices with their start and end apart: 16, of which 9 were waited for; matrix products, arithmetic and copies ran while one was open for 19% of the time, Pallas kernels for 6%

profile of v4, /device:TPU:1, one launch (start us, length us, event | category | flops | bytes accessed | tf_op | source)
XLA Modules:
  0.0 366.0 jit_solution(11645144015420840521)
XLA Ops:
  7.9 5.5 %collective-permute-start = (bf16[640,768]{1,0:T(8,128)(2,1)}, bf16[640,768]{1,0:T(8,128)(2,1)}, u32[]{:S(2)}, u32[]{:S(2)}) collective-permute-start(bf16[640,768]{1,0:T(8,128)(2,1)} %bitcast.102), channel_id=1, source_target_pairs={{0,384},{128,0},{256,128},{384,256},{1,385},{129,1},{257,129},{385... | collective-permute-start | bytes 2949128 | tf_op jit(solution)/shard_map/ppermute | solution.py:145
  16.4 1.5 fusion.10
  17.9 3.2 fusion.4
  21.1 7.0 %all-to-all-start = ((bf16[8,160,768]{2,1,0:T(8,128)(2,1)}), bf16[8,160,768]{2,1,0:T(8,128)(2,1)S(1)}, u32[]{:S(2)}, u32[]{:S(2)}) async-start(bf16[8,160,768]{2,1,0:T(8,128)(2,1)} %bitcast.101), calls=%async_computation | async-start | bytes 3932160 | tf_op jit(solution)/shard_map/all_to_all | solution.py:135
  28.1 1.9 collective-permute-start.1
  30.0 3.6 collective-permute-start.2
  34.9 2.1 broadcast_in_dim.96
  37.0 1.0 constant_dynamic-update-slice_fusion
  38.0 2.2 bitcast_dynamic-update-slice_fusion.2
  40.3 14.6 %collective-permute-done.1 = bf16[640,768]{1,0:T(8,128)(2,1)} collective-permute-done((bf16[640,768]{1,0:T(8,128)(2,1)S(1)}, bf16[640,768]{1,0:T(8,128)(2,1)}, u32[]{:S(2)}, u32[]{:S(2)}) %collective-permute-start.1) | collective-permute-done | bytes 983072 | tf_op jit(solution)/shard_map/ppermute | solution.py:145
  54.8 2.2 bitcast_dynamic-update-slice_fusion.1
  57.1 19.3 %collective-permute-done.2 = bf16[640,768]{1,0:T(8,128)(2,1)} collective-permute-done((bf16[640,768]{1,0:T(8,128)(2,1)S(1)}, bf16[640,768]{1,0:T(8,128)(2,1)}, u32[]{:S(2)}, u32[]{:S(2)}) %collective-permute-start.2) | collective-permute-done | bytes 983072 | tf_op jit(solution)/shard_map/ppermute | solution.py:145
  76.4 2.2 bitcast_dynamic-update-slice_fusion
  78.6 13.3 %all-to-all-start.1 = ((s32[16,1,80]{2,1,0:T(1,128)}), s32[16,1,80]{2,1,0:T(1,128)S(1)}, u32[]{:S(2)}, u32[]{:S(2)}) async-start(s32[16,1,80]{2,1,0:T(1,128)} %bitcast.10), calls=%async_computation.1 | async-start | bytes 16384 | tf_op jit(solution)/shard_map/all_to_all | solution.py:135
  92.0 4.3 %fusion.6 = bf16[1280,768]{1,0:T(8,128)(2,1)} fusion(bf16[1280,768]{1,0:T(8,128)(2,1)S(1)} %bitcast.100, s32[1280]{0:T(1024)S(1)} %copy-done.10), kind=kOutput, calls=%fused_computation.10 | convolution fusion | flops 2519203840 | bytes 3937280 | tf_op jit(solution)/shard_map/dot_general | solution.py:130
  96.2 7.0 %all-to-all-done.1 = s32[16,1,80]{2,1,0:T(1,128)S(1)} async-done(((s32[16,1,80]{2,1,0:T(1,128)}), s32[16,1,80]{2,1,0:T(1,128)S(1)}, u32[]{:S(2)}, u32[]{:S(2)}) %all-to-all-start.1) | async-done | bytes 5152 | tf_op jit(solution)/shard_map/all_to_all | solution.py:135
  105.1 1.4 fusion.9.choose_ref
  106.4 36.3 %all-gather.2.cloned.1.call-done = bf16[2048,2560]{1,0:T(8,128)(2,1)} async-done(((bf16[128,2560]{1,0:T(8,128)(2,1)}), bf16[2048,2560]{1,0:T(8,128)(2,1)}) %all-gather.2.cloned.1.call-update) | async-done | bytes 10485776 | tf_op jit(solution)/shard_map/all_gather | solution.py:165
  142.8 8.6 %all-to-all-start.3 = ((bf16[16,80,768]{2,1,0:T(8,128)(2,1)}), bf16[16,80,768]{2,1,0:T(8,128)(2,1)}, u32[]{:S(2)}, u32[]{:S(2)}) async-start(bf16[16,80,768]{2,1,0:T(8,128)(2,1)} %bitcast.9), calls=%async_computation.3 | async-start | bytes 3932160 | tf_op jit(solution)/shard_map/all_to_all | solution.py:135
  151.6 9.2 %shard_map.85 = (bf16[160,2560]{1,0:T(8,128)(2,1)}, bf16[160,2560]{1,0:T(8,128)(2,1)}, bf16[160,2560]{1,0:T(8,128)(2,1)}, bf16[160,2560]{1,0:T(8,128)(2,1)}, bf1...) custom-call(bf16[4,320,512]{2,1,0:T(8,128)(2,1)} %fusion.9.choose_ref, ...), custom_call_target="tpu_custom_call" | custom-call | flops 3355443200 | bytes 18350080 | tf_op jit(solution)/shard_map/pallas_call | solution.py:45
  160.9 4.7 %collective-permute-start.3 = (bf16[160,2560]{1,0:T(8,128)(2,1)}, bf16[160,2560]{1,0:T(8,128)(2,1)}, u32[]{:S(2)}, u32[]{:S(2)}) collective-permute-start(bf16[160,2560]{1,0:T(8,128)(2,1)} %get-tuple-element.25), channel_id=1, source_target_pairs={{0,64},{1,65},{2,66},{3,67},{4,68},{5,69},{6,70},{7,71},{8,72},{9,... | collective-permute-start | bytes 2457608 | tf_op jit(solution)/shard_map/ppermute | solution.py:191
  165.6 1.7 fusion.2
  167.3 2.2 collective-permute-start.4
  169.6 4.3 %collective-permute-start.5 = (bf16[160,2560]{1,0:T(8,128)(2,1)}, bf16[160,2560]{1,0:T(8,128)(2,1)S(1)}, u32[]{:S(2)}, u32[]{:S(2)}) collective-permute-start(bf16[160,2560]{1,0:T(8,128)(2,1)} %get-tuple-element.27), channel_id=1, source_target_pairs={{0,96},{1,97},{2,98},{3,99},{4,100},{5,101},{6,102},{7,103},{8,104... | collective-permute-start | bytes 2457608 | tf_op jit(solution)/shard_map/ppermute | solution.py:191
  173.9 2.7 collective-permute-start.6
  176.6 2.9 collective-permute-start.7
  179.7 3.0 fusion.14
  182.7 0.9 collective-permute-done.3.refs_1_
  183.6 6.4 %collective-permute-start.8 = (bf16[160,2560]{1,0:T(8,128)(2,1)S(1)}, bf16[160,2560]{1,0:T(8,128)(2,1)S(1)}, u32[]{:S(2)}, u32[]{:S(2)}) collective-permute-start(bf16[160,2560]{1,0:T(8,128)(2,1)S(1)} %copy-done.9), channel_id=1, source_target_pairs={{0,33},{1,32},{2,35},{3,34},{4,37},{5,36},{6,39},{7,38},{8,41},{9,... | collective-permute-start | bytes 2457608 | tf_op jit(solution)/shard_map/ppermute | solution.py:191
  190.0 3.2 fusion.16
  193.2 10.6 %collective-permute-done.4.refs_2_ = bf16[160,2560]{1,0:T(8,128)(2,1)} collective-permute-done((bf16[160,2560]{1,0:T(8,128)(2,1)}, bf16[160,2560]{1,0:T(8,128)(2,1)}, u32[]{:S(2)}, u32[]{:S(2)}) %collective-permute-start.4) | collective-permute-done | bytes 819232 | tf_op jit(solution)/shard_map/ppermute | solution.py:191
  203.8 2.9 collective-permute-start.9
  206.7 3.2 fusion.18
  209.9 3.2 fusion.20
  213.1 8.5 %collective-permute-done.6.refs_4_ = bf16[160,2560]{1,0:T(8,128)(2,1)S(1)} collective-permute-done((bf16[160,2560]{1,0:T(8,128)(2,1)}, bf16[160,2560]{1,0:T(8,128)(2,1)S(1)}, u32[]{:S(2)}, u32[]{:S(2)}) %collective-permute-start.6) | collective-permute-done | bytes 819232 | tf_op jit(solution)/shard_map/ppermute | solution.py:191
  221.6 3.2 fusion.22
  224.9 3.2 fusion.24
  228.1 9.5 %collective-permute-done.8.refs_5_ = bf16[160,2560]{1,0:T(8,128)(2,1)S(1)} collective-permute-done((bf16[160,2560]{1,0:T(8,128)(2,1)S(1)}, bf16[160,2560]{1,0:T(8,128)(2,1)S(1)}, u32[]{:S(2)}, u32[]{:S(2)}) %collective-permute-start.8) | collective-permute-done | bytes 819232 | tf_op jit(solution)/shard_map/ppermute | solution.py:191
  237.7 3.2 fusion.26
  240.9 0.9 copy-done.7
  241.8 2.9 fusion.28
  244.7 1.6 reshape.92
  246.3 15.4 %all-to-all-start.2 = ((bf16[128,15,4,128]{3,2,1,0:T(4,128)(2,1)}), bf16[128,15,4,128]{3,2,1,0:T(4,128)(2,1)S(1)}, u32[]{:S(2)}, u32[]{:S(2)}) async-start(bf16[128,15,4,128]{3,2,1,0:T(4,128)(2,1)} %reshape.92), calls=%async_computation.2 | async-start | bytes 3932160 | tf_op jit(solution)/shard_map/all_to_all | solution.py:135
  261.7 5.8 %fusion.5.refs_8_ = bf16[1280,768]{1,0:T(8,128)(2,1)} fusion(bf16[1280,768]{1,0:T(8,128)(2,1)} %bitcast.32, s32[1280]{0:T(1024)S(1)} %concatenate.13), kind=kOutput, calls=%fused_computation.9 | convolution fusion | flops 2519203840 | bytes 3937280 | tf_op jit(solution)/shard_map/dot_general | solution.py:130
  267.5 12.4 %shard_map.86 = bf16[2560,768]{1,0:T(8,128)(2,1)} custom-call(bf16[160,2560]{1,0:T(8,128)(2,1)} %get-tuple-element.23.refs_0_, bf16[160,2560]{1,0:T(8,128)(2,1)} %collective-permute-done.3.refs_1_, bf16[160,2560]{1,0:T(8,128)(2,1)} %collective-permute-done.4.refs_2_, bf16[160,2560]{1,0:T(8,128)(2,1)} %copy-done.3, bf16[160,2560]{1,0:T(8,128)(2,1)} %copy-done.4, ...), custom_call_target="tpu_custom_call" | custom-call | flops 5033164800 | bytes 12451840 | tf_op jit(solution)/shard_map/pallas_call | solution.py:76
  280.0 71.9 %all-to-all-done.2 = bf16[128,15,4,128]{3,2,1,0:T(4,128)(2,1)S(1)} async-done(((bf16[128,15,4,128]{3,2,1,0:T(4,128)(2,1)}), bf16[128,15,4,128]{3,2,1,0:T(4,128)(2,1)S(1)}, u32[]{:S(2)}, u32[]{:S(2)}) %all-to-all-start.2) | async-done | bytes 1966112 | tf_op jit(solution)/shard_map/all_to_all | solution.py:135
  351.9 1.9 reshape.93
  353.7 5.5 %fusion.11 = (bf16[768]{0:T(1024)(128)(2,1)}, bf16[768,768]{1,0:T(8,128)(2,1)}) fusion(bf16[128,6,768]{2,0,1:T(8,128)(2,1)S(1)} %copy-done, f32[768]{0:T(1024)S(1)} %convert_bitcast_fusion, bf16[768,1280]{1,0:T(8,128)(2,1)} %fusion.2, bf16[1280,768]{1,0:T(8,128)(2,1)} %reshape.93), kind=kOutput, calls=%fused_computation.18 | convolution fusion | flops 1512897792 | bytes 6296064 | tf_op jit(solution)/shard_map/dot_general | solution.py:211
  (59 shorter events, 7.1 us)
Async XLA Ops:
  7.2 135.6 %all-gather.2.cloned.1.call-start = ((), (), s32[]{:S(2)}) async-start(), calls=%async_computation.5 | async-start | bytes 11141120 | tf_op jit(solution)/shard_map/all_gather | solution.py:165
  7.9 30.1 %collective-permute-start = (bf16[640,768]{1,0:T(8,128)(2,1)}, bf16[640,768]{1,0:T(8,128)(2,1)}, u32[]{:S(2)}, u32[]{:S(2)}) collective-permute-start(bf16[640,768]{1,0:T(8,128)(2,1)} %bitcast.102), channel_id=1, source_target_pairs={{0,384},{128,0},{256,128},{384,256},{1,385},{129,1},{257,129},{385... | collective-permute-start | bytes 2949128 | tf_op jit(solution)/shard_map/ppermute | solution.py:145
  21.1 7.0 %copy-start.1 = (bf16[1,640,768]{2,1,0:T(8,128)(2,1)S(1)}, bf16[1,640,768]{2,1,0:T(8,128)(2,1)}, u32[]{:S(2)}) copy-start(bf16[1,640,768]{2,1,0:T(8,128)(2,1)} %param.10) | copy-start | bytes 2949124
  21.1 57.5 %all-to-all-start = ((bf16[8,160,768]{2,1,0:T(8,128)(2,1)}), bf16[8,160,768]{2,1,0:T(8,128)(2,1)S(1)}, u32[]{:S(2)}, u32[]{:S(2)}) async-start(bf16[8,160,768]{2,1,0:T(8,128)(2,1)} %bitcast.101), calls=%async_computation | async-start | bytes 3932160 | tf_op jit(solution)/shard_map/all_to_all | solution.py:135
  28.1 26.8 %collective-permute-start.1 = (bf16[640,768]{1,0:T(8,128)(2,1)S(1)}, bf16[640,768]{1,0:T(8,128)(2,1)}, u32[]{:S(2)}, u32[]{:S(2)}) collective-permute-start(bf16[640,768]{1,0:T(8,128)(2,1)S(1)} %bitcast.103), channel_id=1, source_target_pairs={{0,256},{128,384},{256,0},{384,128},{1,257},{129,385},{257,1},{385... | collective-permute-start | bytes 2949128 | tf_op jit(solution)/shard_map/ppermute | solution.py:145
  30.0 46.4 %collective-permute-start.2 = (bf16[640,768]{1,0:T(8,128)(2,1)S(1)}, bf16[640,768]{1,0:T(8,128)(2,1)}, u32[]{:S(2)}, u32[]{:S(2)}) collective-permute-start(bf16[640,768]{1,0:T(8,128)(2,1)S(1)} %bitcast.104), channel_id=1, source_target_pairs={{0,128},{128,256},{256,384},{384,0},{1,129},{129,257},{257,385},{3... | collective-permute-start | bytes 2949128 | tf_op jit(solution)/shard_map/ppermute | solution.py:145
  40.3 51.7 %copy-start.10 = (s32[1280]{0:T(1024)S(1)}, s32[1280]{0:T(1024)}, u32[]{:S(2)}) copy-start(s32[1280]{0:T(1024)} %constant.287.clone) | copy-start | bytes 15364
  78.6 24.6 %all-to-all-start.1 = ((s32[16,1,80]{2,1,0:T(1,128)}), s32[16,1,80]{2,1,0:T(1,128)S(1)}, u32[]{:S(2)}, u32[]{:S(2)}) async-start(s32[16,1,80]{2,1,0:T(1,128)} %bitcast.10), calls=%async_computation.1 | async-start | bytes 16384 | tf_op jit(solution)/shard_map/all_to_all | solution.py:135
  142.8 103.5 %all-to-all-start.3 = ((bf16[16,80,768]{2,1,0:T(8,128)(2,1)}), bf16[16,80,768]{2,1,0:T(8,128)(2,1)}, u32[]{:S(2)}, u32[]{:S(2)}) async-start(bf16[16,80,768]{2,1,0:T(8,128)(2,1)} %bitcast.9), calls=%async_computation.3 | async-start | bytes 3932160 | tf_op jit(solution)/shard_map/all_to_all | solution.py:135
  160.9 18.8 %copy-start.2 = (bf16[160,2560]{1,0:T(8,128)(2,1)S(1)}, bf16[160,2560]{1,0:T(8,128)(2,1)}, u32[]{:S(2)}) copy-start(bf16[160,2560]{1,0:T(8,128)(2,1)} %get-tuple-element.23.refs_0_) | copy-start | bytes 2457604
  160.9 22.7 %collective-permute-start.3 = (bf16[160,2560]{1,0:T(8,128)(2,1)}, bf16[160,2560]{1,0:T(8,128)(2,1)}, u32[]{:S(2)}, u32[]{:S(2)}) collective-permute-start(bf16[160,2560]{1,0:T(8,128)(2,1)} %get-tuple-element.25), channel_id=1, source_target_pairs={{0,64},{1,65},{2,66},{3,67},{4,68},{5,69},{6,70},{7,71},{8,72},{9,... | collective-permute-start | bytes 2457608 | tf_op jit(solution)/shard_map/ppermute | solution.py:191
  167.3 36.5 %collective-permute-start.4 = (bf16[160,2560]{1,0:T(8,128)(2,1)}, bf16[160,2560]{1,0:T(8,128)(2,1)}, u32[]{:S(2)}, u32[]{:S(2)}) collective-permute-start(bf16[160,2560]{1,0:T(8,128)(2,1)} %get-tuple-element.26), channel_id=1, source_target_pairs={{0,32},{1,33},{2,34},{3,35},{4,36},{5,37},{6,38},{7,39},{8,40},{9,... | collective-permute-start | bytes 2457608 | tf_op jit(solution)/shard_map/ppermute | solution.py:191
  169.6 40.3 %collective-permute-start.5 = (bf16[160,2560]{1,0:T(8,128)(2,1)}, bf16[160,2560]{1,0:T(8,128)(2,1)S(1)}, u32[]{:S(2)}, u32[]{:S(2)}) collective-permute-start(bf16[160,2560]{1,0:T(8,128)(2,1)} %get-tuple-element.27), channel_id=1, source_target_pairs={{0,96},{1,97},{2,98},{3,99},{4,100},{5,101},{6,102},{7,103},{8,104... | collective-permute-start | bytes 2457608 | tf_op jit(solution)/shard_map/ppermute | solution.py:191
  173.9 47.8 %collective-permute-start.6 = (bf16[160,2560]{1,0:T(8,128)(2,1)}, bf16[160,2560]{1,0:T(8,128)(2,1)S(1)}, u32[]{:S(2)}, u32[]{:S(2)}) collective-permute-start(bf16[160,2560]{1,0:T(8,128)(2,1)} %get-tuple-element.28), channel_id=1, source_target_pairs={{0,65},{1,64},{2,67},{3,66},{4,69},{5,68},{6,71},{7,70},{8,73},{9,... | collective-permute-start | bytes 2457608 | tf_op jit(solution)/shard_map/ppermute | solution.py:191
  176.6 48.3 %collective-permute-start.7 = (bf16[160,2560]{1,0:T(8,128)(2,1)}, bf16[160,2560]{1,0:T(8,128)(2,1)S(1)}, u32[]{:S(2)}, u32[]{:S(2)}) collective-permute-start(bf16[160,2560]{1,0:T(8,128)(2,1)} %get-tuple-element.29), channel_id=1, source_target_pairs={{0,1},{1,0},{2,3},{3,2},{4,5},{5,4},{6,7},{7,6},{8,9},{9,8},{10,11... | collective-permute-start | bytes 2457608 | tf_op jit(solution)/shard_map/ppermute | solution.py:191
  179.7 3.9 %copy-start.9 = (bf16[160,2560]{1,0:T(8,128)(2,1)S(1)}, bf16[160,2560]{1,0:T(8,128)(2,1)}, u32[]{:S(2)}) copy-start(bf16[160,2560]{1,0:T(8,128)(2,1)} %get-tuple-element.30) | copy-start | bytes 2457604
  183.6 20.2 %copy-start.8 = (bf16[160,2560]{1,0:T(8,128)(2,1)S(1)}, bf16[160,2560]{1,0:T(8,128)(2,1)}, u32[]{:S(2)}) copy-start(bf16[160,2560]{1,0:T(8,128)(2,1)} %get-tuple-element.31) | copy-start | bytes 2457604
  183.6 54.1 %collective-permute-start.8 = (bf16[160,2560]{1,0:T(8,128)(2,1)S(1)}, bf16[160,2560]{1,0:T(8,128)(2,1)S(1)}, u32[]{:S(2)}, u32[]{:S(2)}) collective-permute-start(bf16[160,2560]{1,0:T(8,128)(2,1)S(1)} %copy-done.9), channel_id=1, source_target_pairs={{0,33},{1,32},{2,35},{3,34},{4,37},{5,36},{6,39},{7,38},{8,41},{9,... | collective-permute-start | bytes 2457608 | tf_op jit(solution)/shard_map/ppermute | solution.py:191
  203.8 37.1 %collective-permute-start.9 = (bf16[160,2560]{1,0:T(8,128)(2,1)S(1)}, bf16[160,2560]{1,0:T(8,128)(2,1)S(1)}, u32[]{:S(2)}, u32[]{:S(2)}) collective-permute-start(bf16[160,2560]{1,0:T(8,128)(2,1)S(1)} %copy-done.8), channel_id=1, source_target_pairs={{0,97},{1,96},{2,99},{3,98},{4,101},{5,100},{6,103},{7,102},{8,105... | collective-permute-start | bytes 2457608 | tf_op jit(solution)/shard_map/ppermute | solution.py:191
  209.9 3.2 copy-start.3
  221.6 3.2 copy-start.4
  224.9 3.2 copy-start.5
  237.7 3.2 copy-start.6
  240.9 0.9 copy-start.7
  246.3 105.6 %all-to-all-start.2 = ((bf16[128,15,4,128]{3,2,1,0:T(4,128)(2,1)}), bf16[128,15,4,128]{3,2,1,0:T(4,128)(2,1)S(1)}, u32[]{:S(2)}, u32[]{:S(2)}) async-start(bf16[128,15,4,128]{3,2,1,0:T(4,128)(2,1)} %reshape.92), calls=%async_computation.2 | async-start | bytes 3932160 | tf_op jit(solution)/shard_map/all_to_all | solution.py:135
  261.7 97.5 %reduce-scatter.2.cloned.1.call-start = ((), (), s32[]{:S(2)}) async-start(), calls=%async_computation.6 | async-start | bytes 4915200 | tf_op jit(solution)/shard_map/reduce_scatter | solution.py:209
  279.9 73.8 %copy-start = (bf16[128,6,768]{2,0,1:T(8,128)(2,1)S(1)}, bf16[128,6,768]{2,0,1:T(8,128)(2,1)}, u32[]{:S(2)}) copy-start(bf16[128,6,768]{2,0,1:T(8,128)(2,1)} %param.7) | copy-start | bytes 3538948
Sparse Core Ops, SparseCore 0:
  10.1 132.6 all-gather.1
  280.1 53.2 reduce-scatter.1

commit v5 on v4

--- a/solution.py
+++ b/solution.py
@@ -10,7 +10,7 @@
 GROUP = 4
 VMEM = 60 * 2**20
 PLACES = ((0, 0), (2, 0), (1, 0), (3, 0), (2, 1), (1, 1), (3, 1), (0, 1))
-DONE_ORDER = (0, 1, 2, 3, 4, 7, 5, 6)
+DONE_ORDER = ((0,), (1,), (2,), (3,), (4,), (7,), (5, 6))
 
 
 def grid_of(dims):
@@ -192,11 +192,12 @@
         work_cot.append(part)
     sources = [(my_x - dx) % nx * nc + (my_c - dc) % nc for dx, dc in PLACES]
     back = jnp.zeros((plane, nz * SLOTS, hidden), jnp.bfloat16)
-    for part in DONE_ORDER:
-        grads = jnp.dot(work_cot[part], weight, preferred_element_type=jnp.float32)
-        back = lax.dynamic_update_index_in_dim(
-            back, grads.astype(jnp.bfloat16), sources[part], 0
-        )
+    for parts in DONE_ORDER:
+        joined = jnp.concatenate([work_cot[part] for part in parts])
+        grads = jnp.dot(joined, weight, preferred_element_type=jnp.float32)
+        grads = grads.astype(jnp.bfloat16).reshape(len(parts), nz * SLOTS, hidden)
+        for at, part in enumerate(parts):
+            back = lax.dynamic_update_index_in_dim(back, grads[at], sources[part], 0)
     take = (by_plane[:, None] == jnp.arange(rows, dtype=jnp.int32)[None, :]).astype(jnp.bfloat16)
     take, back = lax.optimization_barrier((take, back))
     home = swapped(back.reshape(experts, lanes // 4, 4, 128), by_core).reshape(rows, hidden)

time: 371 us -> 369 us (level)
    dot_general x8 -> x7, matrix products: 25.1 us -> 23 us  [on_device(): grads = jnp.dot(joined, weight, preferred_element_type=jnp.float32)]
  transfers between devices with their start and end apart: 16 -> 16, of which waited for: 9 -> 10; matrix products, arithmetic and copies ran while one was open for 19% -> 18% of each run, Pallas kernels for 6% -> 6%
where the time goes in v5:
time: 369 us; the launch traced here: 363 us
  waiting for transfers between devices  179 us (49%)
  starting transfers between devices  81.6 us (22%)
  matrix products  41.8 us (11%)
  Pallas kernels  21.6 us (6%)
  local copies, waits for them, and re-layouts  15.3 us (4%)
  between operations  14.7 us (4%)
  other arithmetic  8.72 us (2%)
    all_to_all x4, waiting for transfers between devices, swapped(): lax.all_to_all(block, 'expert', 0, 0, axis_index_groups=groups, tiled=True)  78.9 us
    all_to_all x4, starting transfers between devices, swapped(): lax.all_to_all(block, 'expert', 0, 0, axis_index_groups=groups, tiled=True)  44.3 us
    all_gather x1, waiting for transfers between devices, on_device(): lax.all_gather(down_cotangent, 'expert', axis_index_groups=along_z, axis=...  36.3 us
    ppermute x3, waiting for transfers between devices, on_device(): lax.ppermute(own, 'dp', [(i, (i - step) % replicas) for i in range(replic...  33.8 us
    ppermute x7, waiting for transfers between devices, on_device(): part = lax.ppermute(part, 'expert', moves)  29.6 us
    ppermute x7, starting transfers between devices, on_device(): part = lax.ppermute(part, 'expert', moves)  26.2 us
    dot_general x7, matrix products, on_device(): grads = jnp.dot(joined, weight, preferred_element_type=jnp.float32)  23 us
    pallas_call x1, Pallas kernels, outer_sum(): pl.pallas_call(outer_kernel, grid=(width // tile,), in_specs=[pl.BlockSpe...  12.4 us
  transfers between devices with their start and end apart: 16, of which 10 were waited for; matrix products, arithmetic and copies ran while one was open for 18% of the time, Pallas kernels for 6%

profile of v5, /device:TPU:1, one launch (start us, length us, event | category | flops | bytes accessed | tf_op | source)
XLA Modules:
  0.0 363.2 jit_solution(9947312655762834362)
XLA Ops:
  7.9 5.5 %collective-permute-start = (bf16[640,768]{1,0:T(8,128)(2,1)}, bf16[640,768]{1,0:T(8,128)(2,1)}, u32[]{:S(2)}, u32[]{:S(2)}) collective-permute-start(bf16[640,768]{1,0:T(8,128)(2,1)} %bitcast.99), channel_id=1, source_target_pairs={{0,384},{128,0},{256,128},{384,256},{1,385},{129,1},{257,129},{385... | collective-permute-start | bytes 2949128 | tf_op jit(solution)/shard_map/ppermute | solution.py:145
  13.4 0.7 fusion.33
  14.3 0.7 select_reduce_fusion.1
  16.4 1.5 fusion.10
  17.9 3.2 fusion.4
  21.1 7.0 %all-to-all-start = ((bf16[8,160,768]{2,1,0:T(8,128)(2,1)}), bf16[8,160,768]{2,1,0:T(8,128)(2,1)S(1)}, u32[]{:S(2)}, u32[]{:S(2)}) async-start(bf16[8,160,768]{2,1,0:T(8,128)(2,1)} %bitcast.98), calls=%async_computation | async-start | bytes 3932160 | tf_op jit(solution)/shard_map/all_to_all | solution.py:135
  28.1 1.9 collective-permute-start.1
  30.0 3.6 %collective-permute-start.2 = (bf16[640,768]{1,0:T(8,128)(2,1)S(1)}, bf16[640,768]{1,0:T(8,128)(2,1)}, u32[]{:S(2)}, u32[]{:S(2)}) collective-permute-start(bf16[640,768]{1,0:T(8,128)(2,1)S(1)} %bitcast.101), channel_id=1, source_target_pairs={{0,128},{128,256},{256,384},{384,0},{1,129},{129,257},{257,385},{3... | collective-permute-start | bytes 2949128 | tf_op jit(solution)/shard_map/ppermute | solution.py:145
  34.9 2.1 broadcast_in_dim.92
  37.0 1.0 constant_dynamic-update-slice_fusion
  38.0 2.2 bitcast_dynamic-update-slice_fusion.2
  40.3 14.6 %collective-permute-done.1 = bf16[640,768]{1,0:T(8,128)(2,1)} collective-permute-done((bf16[640,768]{1,0:T(8,128)(2,1)S(1)}, bf16[640,768]{1,0:T(8,128)(2,1)}, u32[]{:S(2)}, u32[]{:S(2)}) %collective-permute-start.1) | collective-permute-done | bytes 983072 | tf_op jit(solution)/shard_map/ppermute | solution.py:145
  54.8 2.2 bitcast_dynamic-update-slice_fusion.1
  57.1 19.3 %collective-permute-done.2 = bf16[640,768]{1,0:T(8,128)(2,1)} collective-permute-done((bf16[640,768]{1,0:T(8,128)(2,1)S(1)}, bf16[640,768]{1,0:T(8,128)(2,1)}, u32[]{:S(2)}, u32[]{:S(2)}) %collective-permute-start.2) | collective-permute-done | bytes 983072 | tf_op jit(solution)/shard_map/ppermute | solution.py:145
  76.4 2.2 bitcast_dynamic-update-slice_fusion
  78.6 13.3 %all-to-all-start.1 = ((s32[16,1,80]{2,1,0:T(1,128)}), s32[16,1,80]{2,1,0:T(1,128)S(1)}, u32[]{:S(2)}, u32[]{:S(2)}) async-start(s32[16,1,80]{2,1,0:T(1,128)} %bitcast.10), calls=%async_computation.1 | async-start | bytes 16384 | tf_op jit(solution)/shard_map/all_to_all | solution.py:135
  92.0 4.3 %fusion.6 = bf16[1280,768]{1,0:T(8,128)(2,1)} fusion(bf16[1280,768]{1,0:T(8,128)(2,1)S(1)} %bitcast.97, s32[1280]{0:T(1024)S(1)} %copy-done.10), kind=kOutput, calls=%fused_computation.10 | convolution fusion | flops 2519203840 | bytes 3937280 | tf_op jit(solution)/shard_map/dot_general | solution.py:130
  96.2 7.0 %all-to-all-done.1 = s32[16,1,80]{2,1,0:T(1,128)S(1)} async-done(((s32[16,1,80]{2,1,0:T(1,128)}), s32[16,1,80]{2,1,0:T(1,128)S(1)}, u32[]{:S(2)}, u32[]{:S(2)}) %all-to-all-start.1) | async-done | bytes 5152 | tf_op jit(solution)/shard_map/all_to_all | solution.py:135
  105.1 1.4 fusion.9.choose_ref
  106.4 36.3 %all-gather.2.cloned.1.call-done = bf16[2048,2560]{1,0:T(8,128)(2,1)} async-done(((bf16[128,2560]{1,0:T(8,128)(2,1)}), bf16[2048,2560]{1,0:T(8,128)(2,1)}) %all-gather.2.cloned.1.call-update) | async-done | bytes 10485776 | tf_op jit(solution)/shard_map/all_gather | solution.py:165
  142.8 8.6 %all-to-all-start.3 = ((bf16[16,80,768]{2,1,0:T(8,128)(2,1)}), bf16[16,80,768]{2,1,0:T(8,128)(2,1)}, u32[]{:S(2)}, u32[]{:S(2)}) async-start(bf16[16,80,768]{2,1,0:T(8,128)(2,1)} %bitcast.9), calls=%async_computation.3 | async-start | bytes 3932160 | tf_op jit(solution)/shard_map/all_to_all | solution.py:135
  151.6 9.2 %shard_map.85 = (bf16[160,2560]{1,0:T(8,128)(2,1)}, bf16[160,2560]{1,0:T(8,128)(2,1)}, bf16[160,2560]{1,0:T(8,128)(2,1)}, bf16[160,2560]{1,0:T(8,128)(2,1)}, bf1...) custom-call(bf16[4,320,512]{2,1,0:T(8,128)(2,1)} %fusion.9.choose_ref, ...), custom_call_target="tpu_custom_call" | custom-call | flops 3355443200 | bytes 18350080 | tf_op jit(solution)/shard_map/pallas_call | solution.py:45
  160.9 4.7 %collective-permute-start.3 = (bf16[160,2560]{1,0:T(8,128)(2,1)}, bf16[160,2560]{1,0:T(8,128)(2,1)}, u32[]{:S(2)}, u32[]{:S(2)}) collective-permute-start(bf16[160,2560]{1,0:T(8,128)(2,1)} %get-tuple-element.25), channel_id=1, source_target_pairs={{0,64},{1,65},{2,66},{3,67},{4,68},{5,69},{6,70},{7,71},{8,72},{9,... | collective-permute-start | bytes 2457608 | tf_op jit(solution)/shard_map/ppermute | solution.py:191
  165.6 1.7 fusion.2
  167.3 2.2 collective-permute-start.4
  169.6 4.3 %collective-permute-start.5 = (bf16[160,2560]{1,0:T(8,128)(2,1)}, bf16[160,2560]{1,0:T(8,128)(2,1)S(1)}, u32[]{:S(2)}, u32[]{:S(2)}) collective-permute-start(bf16[160,2560]{1,0:T(8,128)(2,1)} %get-tuple-element.27), channel_id=1, source_target_pairs={{0,96},{1,97},{2,98},{3,99},{4,100},{5,101},{6,102},{7,103},{8,104... | collective-permute-start | bytes 2457608 | tf_op jit(solution)/shard_map/ppermute | solution.py:191
  173.9 2.7 collective-permute-start.6
  176.6 2.9 collective-permute-start.7
  179.7 3.0 fusion.21
  182.7 0.9 collective-permute-done.3.refs_1_
  183.6 6.4 %collective-permute-start.8 = (bf16[160,2560]{1,0:T(8,128)(2,1)S(1)}, bf16[160,2560]{1,0:T(8,128)(2,1)S(1)}, u32[]{:S(2)}, u32[]{:S(2)}) collective-permute-start(bf16[160,2560]{1,0:T(8,128)(2,1)S(1)} %copy-done.7), channel_id=1, source_target_pairs={{0,33},{1,32},{2,35},{3,34},{4,37},{5,36},{6,39},{7,38},{8,41},{9,... | collective-permute-start | bytes 2457608 | tf_op jit(solution)/shard_map/ppermute | solution.py:191
  190.0 3.2 fusion.23
  193.2 10.6 %collective-permute-done.4.refs_2_ = bf16[160,2560]{1,0:T(8,128)(2,1)} collective-permute-done((bf16[160,2560]{1,0:T(8,128)(2,1)}, bf16[160,2560]{1,0:T(8,128)(2,1)}, u32[]{:S(2)}, u32[]{:S(2)}) %collective-permute-start.4) | collective-permute-done | bytes 819232 | tf_op jit(solution)/shard_map/ppermute | solution.py:191
  203.8 2.9 collective-permute-start.9
  206.7 3.2 fusion.25
  209.9 3.2 fusion.27
  213.1 8.5 %collective-permute-done.6.refs_4_ = bf16[160,2560]{1,0:T(8,128)(2,1)S(1)} collective-permute-done((bf16[160,2560]{1,0:T(8,128)(2,1)}, bf16[160,2560]{1,0:T(8,128)(2,1)S(1)}, u32[]{:S(2)}, u32[]{:S(2)}) %collective-permute-start.6) | collective-permute-done | bytes 819232 | tf_op jit(solution)/shard_map/ppermute | solution.py:191
  221.6 3.2 fusion.29
  224.9 3.2 fusion.31
  228.1 9.5 %collective-permute-done.8.refs_5_ = bf16[160,2560]{1,0:T(8,128)(2,1)S(1)} collective-permute-done((bf16[160,2560]{1,0:T(8,128)(2,1)S(1)}, bf16[160,2560]{1,0:T(8,128)(2,1)S(1)}, u32[]{:S(2)}, u32[]{:S(2)}) %collective-permute-start.8) | collective-permute-done | bytes 819232 | tf_op jit(solution)/shard_map/ppermute | solution.py:191
  237.8 4.0 %fusion.17 = bf16[320,768]{1,0:T(8,128)(2,1)S(1)} fusion(bf16[2560,768]{1,0:T(8,128)(2,1)} %bitcast.17, bf16[160,2560]{1,0:T(8,128)(2,1)S(1)} %collective-permute-done.9.refs_6_, bf16[160,2560]{1,0:T(8,128)(2,1)S(1)} %collective-permute-done.8.refs_5_), kind=kOutput, calls=%fused_computation.25 | convolution fusion | flops 1261813760 | bytes 6062080 | tf_op jit(solution)/shard_map/dot_general | solution.py:197
  241.9 1.6 reshape.95
  243.5 15.4 %all-to-all-start.2 = ((bf16[128,15,4,128]{3,2,1,0:T(4,128)(2,1)}), bf16[128,15,4,128]{3,2,1,0:T(4,128)(2,1)S(1)}, u32[]{:S(2)}, u32[]{:S(2)}) async-start(bf16[128,15,4,128]{3,2,1,0:T(4,128)(2,1)} %reshape.95), calls=%async_computation.2 | async-start | bytes 3932160 | tf_op jit(solution)/shard_map/all_to_all | solution.py:135
  258.9 5.8 %fusion.5.refs_8_ = bf16[1280,768]{1,0:T(8,128)(2,1)} fusion(bf16[1280,768]{1,0:T(8,128)(2,1)} %bitcast.32, s32[1280]{0:T(1024)S(1)} %concatenate.17), kind=kOutput, calls=%fused_computation.9 | convolution fusion | flops 2519203840 | bytes 3937280 | tf_op jit(solution)/shard_map/dot_general | solution.py:130
  264.7 12.4 %shard_map.86 = bf16[2560,768]{1,0:T(8,128)(2,1)} custom-call(bf16[160,2560]{1,0:T(8,128)(2,1)} %get-tuple-element.23.refs_0_, bf16[160,2560]{1,0:T(8,128)(2,1)} %collective-permute-done.3.refs_1_, bf16[160,2560]{1,0:T(8,128)(2,1)} %collective-permute-done.4.refs_2_, bf16[160,2560]{1,0:T(8,128)(2,1)} %copy-done.3, bf16[160,2560]{1,0:T(8,128)(2,1)} %copy-done.4, ...), custom_call_target="tpu_custom_call" | custom-call | flops 5033164800 | bytes 12451840 | tf_op jit(solution)/shard_map/pallas_call | solution.py:76
  277.1 71.9 %all-to-all-done.2 = bf16[128,15,4,128]{3,2,1,0:T(4,128)(2,1)S(1)} async-done(((bf16[128,15,4,128]{3,2,1,0:T(4,128)(2,1)}), bf16[128,15,4,128]{3,2,1,0:T(4,128)(2,1)S(1)}, u32[]{:S(2)}, u32[]{:S(2)}) %all-to-all-start.2) | async-done | bytes 1966112 | tf_op jit(solution)/shard_map/all_to_all | solution.py:135
  349.0 1.9 reshape.96
  350.9 5.4 %fusion.11 = (bf16[768]{0:T(1024)(128)(2,1)}, bf16[768,768]{1,0:T(8,128)(2,1)}) fusion(bf16[128,6,768]{2,0,1:T(8,128)(2,1)S(1)} %copy-done, f32[768]{0:T(1024)S(1)} %convert_bitcast_fusion, bf16[768,1280]{1,0:T(8,128)(2,1)} %fusion.2, bf16[1280,768]{1,0:T(8,128)(2,1)} %reshape.96), kind=kOutput, calls=%fused_computation.18 | convolution fusion | flops 1512897792 | bytes 6296064 | tf_op jit(solution)/shard_map/dot_general | solution.py:212
  (60 shorter events, 5.7 us)
Async XLA Ops:
  7.2 135.6 %all-gather.2.cloned.1.call-start = ((), (), s32[]{:S(2)}) async-start(), calls=%async_computation.5 | async-start | bytes 11141120 | tf_op jit(solution)/shard_map/all_gather | solution.py:165
  7.9 30.1 %collective-permute-start = (bf16[640,768]{1,0:T(8,128)(2,1)}, bf16[640,768]{1,0:T(8,128)(2,1)}, u32[]{:S(2)}, u32[]{:S(2)}) collective-permute-start(bf16[640,768]{1,0:T(8,128)(2,1)} %bitcast.99), channel_id=1, source_target_pairs={{0,384},{128,0},{256,128},{384,256},{1,385},{129,1},{257,129},{385... | collective-permute-start | bytes 2949128 | tf_op jit(solution)/shard_map/ppermute | solution.py:145
  21.1 7.0 %copy-start.1 = (bf16[1,640,768]{2,1,0:T(8,128)(2,1)S(1)}, bf16[1,640,768]{2,1,0:T(8,128)(2,1)}, u32[]{:S(2)}) copy-start(bf16[1,640,768]{2,1,0:T(8,128)(2,1)} %param.10) | copy-start | bytes 2949124
  21.1 57.5 %all-to-all-start = ((bf16[8,160,768]{2,1,0:T(8,128)(2,1)}), bf16[8,160,768]{2,1,0:T(8,128)(2,1)S(1)}, u32[]{:S(2)}, u32[]{:S(2)}) async-start(bf16[8,160,768]{2,1,0:T(8,128)(2,1)} %bitcast.98), calls=%async_computation | async-start | bytes 3932160 | tf_op jit(solution)/shard_map/all_to_all | solution.py:135
  28.1 26.8 %collective-permute-start.1 = (bf16[640,768]{1,0:T(8,128)(2,1)S(1)}, bf16[640,768]{1,0:T(8,128)(2,1)}, u32[]{:S(2)}, u32[]{:S(2)}) collective-permute-start(bf16[640,768]{1,0:T(8,128)(2,1)S(1)} %bitcast.100), channel_id=1, source_target_pairs={{0,256},{128,384},{256,0},{384,128},{1,257},{129,385},{257,1},{385... | collective-permute-start | bytes 2949128 | tf_op jit(solution)/shard_map/ppermute | solution.py:145
  30.0 46.4 %collective-permute-start.2 = (bf16[640,768]{1,0:T(8,128)(2,1)S(1)}, bf16[640,768]{1,0:T(8,128)(2,1)}, u32[]{:S(2)}, u32[]{:S(2)}) collective-permute-start(bf16[640,768]{1,0:T(8,128)(2,1)S(1)} %bitcast.101), channel_id=1, source_target_pairs={{0,128},{128,256},{256,384},{384,0},{1,129},{129,257},{257,385},{3... | collective-permute-start | bytes 2949128 | tf_op jit(solution)/shard_map/ppermute | solution.py:145
  40.3 51.7 %copy-start.10 = (s32[1280]{0:T(1024)S(1)}, s32[1280]{0:T(1024)}, u32[]{:S(2)}) copy-start(s32[1280]{0:T(1024)} %constant.287.clone) | copy-start | bytes 15364
  78.6 24.6 %all-to-all-start.1 = ((s32[16,1,80]{2,1,0:T(1,128)}), s32[16,1,80]{2,1,0:T(1,128)S(1)}, u32[]{:S(2)}, u32[]{:S(2)}) async-start(s32[16,1,80]{2,1,0:T(1,128)} %bitcast.10), calls=%async_computation.1 | async-start | bytes 16384 | tf_op jit(solution)/shard_map/all_to_all | solution.py:135
  142.8 100.7 %all-to-all-start.3 = ((bf16[16,80,768]{2,1,0:T(8,128)(2,1)}), bf16[16,80,768]{2,1,0:T(8,128)(2,1)}, u32[]{:S(2)}, u32[]{:S(2)}) async-start(bf16[16,80,768]{2,1,0:T(8,128)(2,1)} %bitcast.9), calls=%async_computation.3 | async-start | bytes 3932160 | tf_op jit(solution)/shard_map/all_to_all | solution.py:135
  160.9 18.8 %copy-start.2 = (bf16[160,2560]{1,0:T(8,128)(2,1)S(1)}, bf16[160,2560]{1,0:T(8,128)(2,1)}, u32[]{:S(2)}) copy-start(bf16[160,2560]{1,0:T(8,128)(2,1)} %get-tuple-element.23.refs_0_) | copy-start | bytes 2457604
  160.9 22.7 %collective-permute-start.3 = (bf16[160,2560]{1,0:T(8,128)(2,1)}, bf16[160,2560]{1,0:T(8,128)(2,1)}, u32[]{:S(2)}, u32[]{:S(2)}) collective-permute-start(bf16[160,2560]{1,0:T(8,128)(2,1)} %get-tuple-element.25), channel_id=1, source_target_pairs={{0,64},{1,65},{2,66},{3,67},{4,68},{5,69},{6,70},{7,71},{8,72},{9,... | collective-permute-start | bytes 2457608 | tf_op jit(solution)/shard_map/ppermute | solution.py:191
  167.3 36.5 %collective-permute-start.4 = (bf16[160,2560]{1,0:T(8,128)(2,1)}, bf16[160,2560]{1,0:T(8,128)(2,1)}, u32[]{:S(2)}, u32[]{:S(2)}) collective-permute-start(bf16[160,2560]{1,0:T(8,128)(2,1)} %get-tuple-element.26), channel_id=1, source_target_pairs={{0,32},{1,33},{2,34},{3,35},{4,36},{5,37},{6,38},{7,39},{8,40},{9,... | collective-permute-start | bytes 2457608 | tf_op jit(solution)/shard_map/ppermute | solution.py:191
  169.6 40.3 %collective-permute-start.5 = (bf16[160,2560]{1,0:T(8,128)(2,1)}, bf16[160,2560]{1,0:T(8,128)(2,1)S(1)}, u32[]{:S(2)}, u32[]{:S(2)}) collective-permute-start(bf16[160,2560]{1,0:T(8,128)(2,1)} %get-tuple-element.27), channel_id=1, source_target_pairs={{0,96},{1,97},{2,98},{3,99},{4,100},{5,101},{6,102},{7,103},{8,104... | collective-permute-start | bytes 2457608 | tf_op jit(solution)/shard_map/ppermute | solution.py:191
  173.9 47.8 %collective-permute-start.6 = (bf16[160,2560]{1,0:T(8,128)(2,1)}, bf16[160,2560]{1,0:T(8,128)(2,1)S(1)}, u32[]{:S(2)}, u32[]{:S(2)}) collective-permute-start(bf16[160,2560]{1,0:T(8,128)(2,1)} %get-tuple-element.28), channel_id=1, source_target_pairs={{0,65},{1,64},{2,67},{3,66},{4,69},{5,68},{6,71},{7,70},{8,73},{9,... | collective-permute-start | bytes 2457608 | tf_op jit(solution)/shard_map/ppermute | solution.py:191
  176.6 48.3 %collective-permute-start.7 = (bf16[160,2560]{1,0:T(8,128)(2,1)}, bf16[160,2560]{1,0:T(8,128)(2,1)S(1)}, u32[]{:S(2)}, u32[]{:S(2)}) collective-permute-start(bf16[160,2560]{1,0:T(8,128)(2,1)} %get-tuple-element.29), channel_id=1, source_target_pairs={{0,1},{1,0},{2,3},{3,2},{4,5},{5,4},{6,7},{7,6},{8,9},{9,8},{10,11... | collective-permute-start | bytes 2457608 | tf_op jit(solution)/shard_map/ppermute | solution.py:191
  179.7 3.9 %copy-start.7 = (bf16[160,2560]{1,0:T(8,128)(2,1)S(1)}, bf16[160,2560]{1,0:T(8,128)(2,1)}, u32[]{:S(2)}) copy-start(bf16[160,2560]{1,0:T(8,128)(2,1)} %get-tuple-element.30) | copy-start | bytes 2457604
  183.6 20.2 %copy-start.6 = (bf16[160,2560]{1,0:T(8,128)(2,1)S(1)}, bf16[160,2560]{1,0:T(8,128)(2,1)}, u32[]{:S(2)}) copy-start(bf16[160,2560]{1,0:T(8,128)(2,1)} %get-tuple-element.31) | copy-start | bytes 2457604
  183.6 54.1 %collective-permute-start.8 = (bf16[160,2560]{1,0:T(8,128)(2,1)S(1)}, bf16[160,2560]{1,0:T(8,128)(2,1)S(1)}, u32[]{:S(2)}, u32[]{:S(2)}) collective-permute-start(bf16[160,2560]{1,0:T(8,128)(2,1)S(1)} %copy-done.7), channel_id=1, source_target_pairs={{0,33},{1,32},{2,35},{3,34},{4,37},{5,36},{6,39},{7,38},{8,41},{9,... | collective-permute-start | bytes 2457608 | tf_op jit(solution)/shard_map/ppermute | solution.py:191
  203.8 34.0 %collective-permute-start.9 = (bf16[160,2560]{1,0:T(8,128)(2,1)S(1)}, bf16[160,2560]{1,0:T(8,128)(2,1)S(1)}, u32[]{:S(2)}, u32[]{:S(2)}) collective-permute-start(bf16[160,2560]{1,0:T(8,128)(2,1)S(1)} %copy-done.6), channel_id=1, source_target_pairs={{0,97},{1,96},{2,99},{3,98},{4,101},{5,100},{6,103},{7,102},{8,105... | collective-permute-start | bytes 2457608 | tf_op jit(solution)/shard_map/ppermute | solution.py:191
  209.9 3.2 copy-start.3
  221.6 3.2 copy-start.4
  224.9 3.2 copy-start.5
  237.7 4.2 %copy-start.8 = (bf16[160,2560]{1,0:T(8,128)(2,1)}, bf16[160,2560]{1,0:T(8,128)(2,1)S(1)}, u32[]{:S(2)}) copy-start(bf16[160,2560]{1,0:T(8,128)(2,1)S(1)} %collective-permute-done.8.refs_5_) | copy-start | bytes 2457604
  237.8 4.1 %copy-start.9 = (bf16[160,2560]{1,0:T(8,128)(2,1)}, bf16[160,2560]{1,0:T(8,128)(2,1)S(1)}, u32[]{:S(2)}) copy-start(bf16[160,2560]{1,0:T(8,128)(2,1)S(1)} %collective-permute-done.9.refs_6_) | copy-start | bytes 2457604
  243.5 105.6 %all-to-all-start.2 = ((bf16[128,15,4,128]{3,2,1,0:T(4,128)(2,1)}), bf16[128,15,4,128]{3,2,1,0:T(4,128)(2,1)S(1)}, u32[]{:S(2)}, u32[]{:S(2)}) async-start(bf16[128,15,4,128]{3,2,1,0:T(4,128)(2,1)} %reshape.95), calls=%async_computation.2 | async-start | bytes 3932160 | tf_op jit(solution)/shard_map/all_to_all | solution.py:135
  258.8 97.5 %reduce-scatter.2.cloned.1.call-start = ((), (), s32[]{:S(2)}) async-start(), calls=%async_computation.6 | async-start | bytes 4915200 | tf_op jit(solution)/shard_map/reduce_scatter | solution.py:210
  277.1 73.8 %copy-start = (bf16[128,6,768]{2,0,1:T(8,128)(2,1)S(1)}, bf16[128,6,768]{2,0,1:T(8,128)(2,1)}, u32[]{:S(2)}) copy-start(bf16[128,6,768]{2,0,1:T(8,128)(2,1)} %param.7) | copy-start | bytes 3538948
Sparse Core Ops, SparseCore 0:
  10.1 132.6 all-gather.1
  277.2 53.2 reduce-scatter.1
